TPU v7x, 512 devices: a whole 4x4x16 slice. The times are simulated.
512 devices in a mesh: grp: 16 (over x, y_hi, core), ep: 32 (over y_lo, z).
Axes of the slice: x: 4, y: 4 (y_hi: 2, y_lo: 2; y = y_hi * 2 + y_lo), z: 16, core: 2. Of those that a mesh axis runs over, the one named last changes fastest.
Arguments:
- tokens: bfloat16 [4096, 3584], P('ep', 'grp'), may hold values from -6 to 6
- routes: int32 [4096, 1], P('ep'), may hold values from 0 to 31; in each aligned block of 128 rows (0 to 127, 128 to 255, ...) at most 8 rows name the same one
- route_weights: float32 [4096, 1], P('ep'), may hold values from 0.2 to 1
- hot_experts: int32 [16], replicated, may hold values from 0 to 15, as said below
- w_gate: bfloat16 [16, 3584, 2048], P(None, 'ep', 'grp'), may hold values from -0.09375 to 0.09375
- w_up: bfloat16 [16, 3584, 2048], P(None, 'ep', 'grp'), may hold values from -0.09375 to 0.09375
- w_down: bfloat16 [16, 2048, 3584], P(None, 'grp', 'ep'), may hold values from -0.125 to 0.125
- cotangent: bfloat16 [4096, 3584], P('ep', 'grp'), may hold values from -3 to 3
Outputs:
- layer_output: bfloat16 [4096, 3584], P('ep', 'grp')
- grad_tokens: bfloat16 [4096, 3584], P('ep', 'grp')
- grad_gate: bfloat16 [16, 3584, 2048], P(None, 'ep', 'grp')
- grad_up: bfloat16 [16, 3584, 2048], P(None, 'ep', 'grp')
- grad_down: bfloat16 [16, 2048, 3584], P(None, 'grp', 'ep')
Inputs may be any that keep to these rules, and one draw needn't show every extreme that they name: `routes`: each row names one slot. Among the rows of one device (aligned blocks of 128 rows) no slot is named by more than 8 rows. `hot_experts`: entry j is the expert held by slot 16 + j; an expert may appear several times.
All inputs are finite; a program needn't handle non-finite values.
Results may differ from a plain program's by a relative error of at most 0.02.
Values may be sent and summed in bfloat16 or wider, within the bound.
A program may use at most 64 MiB of HBM per device.

v0:
```python
import jax
import jax.numpy as jnp
from jax import lax
from jax.sharding import PartitionSpec as P


def shards(tokens, routes, route_weights, hot_experts, w_gate, w_up, w_down, cotangent):
    ep_size = lax.axis_size("ep")
    tok_count = tokens.shape[0]
    top_count = routes.shape[1]
    flat_count = tok_count * top_count
    capacity = 2 * flat_count // ep_size
    pad_rows = ep_size * capacity
    expert_count = w_gate.shape[0]
    hidden = w_gate.shape[2]
    stored = w_gate.shape[1]
    width = stored * ep_size
    slot_host = jnp.concatenate([jnp.arange(expert_count, dtype=jnp.int32), hot_experts])
    flat_slot = routes.reshape(-1)
    onehot = (flat_slot[:, None] == jnp.arange(ep_size, dtype=jnp.int32)[None, :]).astype(jnp.int32)
    before = jnp.cumsum(onehot, axis=0) - onehot
    position = jnp.sum(before * onehot, axis=1)
    dest = flat_slot * capacity + position
    source = (
        jnp.full((pad_rows,), flat_count, jnp.int32)
        .at[dest]
        .set(jnp.arange(flat_count, dtype=jnp.int32))
    )
    token_of = source // top_count
    flat_weights = route_weights.reshape(-1)
    weight_of = jnp.take(jnp.concatenate([flat_weights, jnp.zeros((1,), jnp.float32)]), source)
    sel_gate = jnp.take(w_gate, slot_host, axis=0)
    sel_up = jnp.take(w_up, slot_host, axis=0)
    sel_down = jnp.swapaxes(jnp.take(w_down, slot_host, axis=0), 1, 2)
    packed = jnp.concatenate([sel_gate, sel_up, sel_down], axis=2)
    received = lax.all_to_all(packed, "ep", split_axis=0, concat_axis=0, tiled=True)
    slot_weights = received.reshape(width, 3 * hidden)
    gate_up_w = slot_weights[:, : 2 * hidden]
    down_t = slot_weights[:, 2 * hidden :]

    def pick_rows(source_table, route_scale):
        extended = jnp.concatenate(
            [source_table, jnp.zeros((1, source_table.shape[1]), source_table.dtype)], axis=0
        )
        picked = jnp.take(extended, token_of, axis=0)
        if route_scale is not None:
            picked = (picked.astype(jnp.float32) * route_scale[:, None]).astype(jnp.bfloat16)
        return picked

    def deliver(source_table, route_scale):
        send_rows = pick_rows(source_table, route_scale)
        moved = lax.all_to_all(
            send_rows.reshape(ep_size, capacity, -1), "ep", split_axis=0, concat_axis=0, tiled=True
        )
        return lax.all_gather(moved.reshape(pad_rows, -1), "grp", axis=1, tiled=True)

    def combine(part_rows, weighted):
        block_sum = lax.psum_scatter(
            part_rows.astype(jnp.float32).astype(jnp.bfloat16),
            "grp",
            scatter_dimension=1,
            tiled=True,
        ).astype(jnp.float32)
        returned = lax.all_to_all(
            block_sum.reshape(ep_size, capacity, -1).astype(jnp.bfloat16),
            "ep",
            split_axis=0,
            concat_axis=0,
            tiled=True,
        ).astype(jnp.float32)
        route_rows = jnp.take(returned.reshape(pad_rows, -1), dest, axis=0)
        if weighted:
            route_rows = route_rows * flat_weights[:, None]
        return jnp.sum(route_rows.reshape(tok_count, top_count, -1), axis=1)

    contract_last = (((1,), (1,)), ((), ()))
    contract_first = (((0,), (0,)), ((), ()))
    x_rows = deliver(tokens, None)
    gate_up = jnp.dot(x_rows, gate_up_w, preferred_element_type=jnp.float32)
    gate_pre = gate_up[:, :hidden]
    up_pre = gate_up[:, hidden:]
    sigmoid_gate = jax.nn.sigmoid(gate_pre)
    act = (gate_pre * sigmoid_gate * up_pre).astype(jnp.bfloat16)
    out_parts = lax.dot_general(
        act, down_t, contract_last, preferred_element_type=jnp.float32
    ).astype(jnp.bfloat16)
    layer_output = combine(out_parts, True).astype(jnp.bfloat16)
    dz_rows = deliver(cotangent, weight_of)
    act_grad = jnp.dot(dz_rows, down_t, preferred_element_type=jnp.float32)
    gate_grad = act_grad * up_pre * sigmoid_gate * (1.0 + gate_pre * (1.0 - sigmoid_gate))
    up_grad = act_grad * gate_pre * sigmoid_gate
    pre_grad = jnp.concatenate([gate_grad, up_grad], axis=1).astype(jnp.bfloat16)
    tok_parts = lax.dot_general(
        pre_grad, gate_up_w, contract_last, preferred_element_type=jnp.float32
    ).astype(jnp.bfloat16)
    grad_tokens = combine(tok_parts, False).astype(jnp.bfloat16)
    grad_gate_up = lax.dot_general(
        x_rows, pre_grad, contract_first, preferred_element_type=jnp.float32
    )
    grad_down_t = lax.dot_general(dz_rows, act, contract_first, preferred_element_type=jnp.float32)
    slot_grad = jnp.concatenate([grad_gate_up, grad_down_t], axis=1).astype(jnp.bfloat16)
    owner_pieces = lax.all_to_all(
        slot_grad.reshape(ep_size, stored, 3 * hidden),
        "ep",
        split_axis=0,
        concat_axis=0,
        tiled=True,
    )
    host_onehot = (slot_host[None, :] == jnp.arange(expert_count, dtype=jnp.int32)[:, None]).astype(
        jnp.bfloat16
    )
    totals = jnp.einsum(
        "es,sdh->edh", host_onehot, owner_pieces, preferred_element_type=jnp.float32
    )
    grad_gate = totals[:, :, :hidden].astype(jnp.bfloat16)
    grad_up = totals[:, :, hidden : 2 * hidden].astype(jnp.bfloat16)
    grad_down = jnp.swapaxes(totals[:, :, 2 * hidden :], 1, 2).astype(jnp.bfloat16)
    return (layer_output, grad_tokens, grad_gate, grad_up, grad_down)


def solution(mesh):
    placed = (
        P("ep", "grp"),
        P("ep", None),
        P("ep", None),
        P(),
        P(None, "ep", "grp"),
        P(None, "ep", "grp"),
        P(None, "grp", "ep"),
        P("ep", "grp"),
    )
    return jax.shard_map(
        shards,
        mesh=mesh,
        in_specs=placed,
        out_specs=(
            P("ep", "grp"),
            P("ep", "grp"),
            P(None, "ep", "grp"),
            P(None, "ep", "grp"),
            P(None, "grp", "ep"),
        ),
        check_vma=False,
    )
```

profile of v0, /device:TPU:32, one launch (start us, length us, event | category | flops | bytes accessed | tf_op | source)
XLA Modules:
  0.0 573.1 jit_solution(13646672877807859614)
XLA Ops:
  11.4 1.9 gather_fusion.1
  16.2 16.4 %all-to-all-start = ((bf16[32,8,224]{2,1,0:T(8,128)(2,1)}), bf16[32,8,224]{2,1,0:T(8,128)(2,1)S(1)}, u32[]{:S(2)}, u32[]{:S(2)}) async-start(bf16[32,8,224]{2,1,0:T(8,128)(2,1)} %select_bitcast_fusion.1), calls=%async_computation | async-start | bytes 262144 | tf_op jit(solution)/shard_map/all_to_all | solution.py:52
  39.6 8.8 %all-to-all-done = bf16[32,8,224]{2,1,0:T(8,128)(2,1)S(1)} async-done(((bf16[32,8,224]{2,1,0:T(8,128)(2,1)}), bf16[32,8,224]{2,1,0:T(8,128)(2,1)S(1)}, u32[]{:S(2)}, u32[]{:S(2)}) %all-to-all-start) | async-done | bytes 114720 | tf_op jit(solution)/shard_map/all_to_all | solution.py:52
  48.4 4.7 all-to-all-start.3
  53.3 3.4 pad_maximum_fusion
  56.7 11.4 %all-to-all-done.3 = bf16[32,8,224]{2,1,0:T(8,128)(2,1)S(1)} async-done(((bf16[32,8,224]{2,1,0:T(8,128)(2,1)}), bf16[32,8,224]{2,1,0:T(8,128)(2,1)S(1)}, u32[]{:S(2)}, u32[]{:S(2)}) %all-to-all-start.3) | async-done | bytes 114720 | tf_op jit(solution)/shard_map/all_to_all | solution.py:52
  68.1 4.9 all-to-all-start.1
  74.8 69.1 %all-gather.3.cloned.1.call-done = bf16[256,3584]{0,1:T(8,128)(2,1)} async-done(((bf16[256,224]{0,1:T(8,128)(2,1)}), bf16[256,3584]{0,1:T(8,128)(2,1)}) %all-gather.3.cloned.1.call-update) | async-done | bytes 1835024 | tf_op jit(solution)/shard_map/all_gather | solution.py:55
  143.9 53.7 %all-to-all-done.1 = bf16[32,112,384]{2,1,0:T(8,128)(2,1)S(1)} async-done(((bf16[32,112,384]{2,1,0:T(8,128)(2,1)}), bf16[32,112,384]{2,1,0:T(8,128)(2,1)S(1)}, u32[]{:S(2)}, u32[]{:S(2)}) %all-to-all-start.1) | async-done | bytes 2752544 | tf_op jit(solution)/shard_map/all_to_all | solution.py:36
  197.6 3.0 fusion.6
  200.6 10.0 %all-gather.5.cloned.1.call-done = bf16[256,3584]{0,1:T(8,128)(2,1)} async-done(((bf16[256,224]{0,1:T(8,128)(2,1)}), bf16[256,3584]{0,1:T(8,128)(2,1)}) %all-gather.5.cloned.1.call-update) | async-done | bytes 1835024 | tf_op jit(solution)/shard_map/all_gather | solution.py:55
  210.6 2.1 multiply_convert_fusion.2
  212.7 1.9 convolution_convert_fusion.1
  214.7 1.9 convolution_convert_fusion
  216.6 89.9 %reduce-scatter.5.cloned.1.call-done = bf16[256,224]{0,1:T(8,128)(2,1)} async-done(((bf16[256,3584]{0,1:T(8,128)(2,1)}), bf16[256,224]{0,1:T(8,128)(2,1)}) %reduce-scatter.5.cloned.1.call-update) | async-done | bytes 114704 | tf_op jit(solution)/shard_map/reduce_scatter | solution.py:58
  308.2 13.0 %all-to-all-start.4 = ((bf16[32,8,224]{2,1,0:T(8,128)(2,1)}), bf16[32,8,224]{2,1,0:T(8,128)(2,1)S(1)}, u32[]{:S(2)}, u32[]{:S(2)}) async-start(bf16[32,8,224]{2,1,0:T(8,128)(2,1)} %bitcast.14), calls=%async_computation.6 | async-start | bytes 262144 | tf_op jit(solution)/shard_map/all_to_all | solution.py:64
  321.2 2.2 convolution_convert_fusion.2
  323.3 80.7 %reduce-scatter.3.cloned.1.call-done = bf16[256,224]{0,1:T(8,128)(2,1)} async-done(((bf16[256,3584]{0,1:T(8,128)(2,1)}), bf16[256,224]{0,1:T(8,128)(2,1)}) %reduce-scatter.3.cloned.1.call-update) | async-done | bytes 114704 | tf_op jit(solution)/shard_map/reduce_scatter | solution.py:58
  405.7 13.0 %all-to-all-start.2 = ((bf16[32,8,224]{2,1,0:T(8,128)(2,1)}), bf16[32,8,224]{2,1,0:T(8,128)(2,1)S(1)}, u32[]{:S(2)}, u32[]{:S(2)}) async-start(bf16[32,8,224]{2,1,0:T(8,128)(2,1)} %bitcast.9), calls=%async_computation.3 | async-start | bytes 262144 | tf_op jit(solution)/shard_map/all_to_all | solution.py:64
  418.8 2.1 convolution_convert_fusion.3
  420.9 1.8 pad_maximum_fusion.1
  422.7 10.6 %all-to-all-done.2 = bf16[32,8,224]{2,1,0:T(8,128)(2,1)S(1)} async-done(((bf16[32,8,224]{2,1,0:T(8,128)(2,1)}), bf16[32,8,224]{2,1,0:T(8,128)(2,1)S(1)}, u32[]{:S(2)}, u32[]{:S(2)}) %all-to-all-start.2) | async-done | bytes 114720 | tf_op jit(solution)/shard_map/all_to_all | solution.py:64
  434.0 4.9 all-to-all-start.5
  444.7 118.4 %all-to-all-done.5 = bf16[32,112,384]{2,1,0:T(8,128)(2,1)S(1)} async-done(((bf16[32,112,384]{2,1,0:T(8,128)(2,1)}), bf16[32,112,384]{2,1,0:T(8,128)(2,1)S(1)}, u32[]{:S(2)}, u32[]{:S(2)}) %all-to-all-start.5) | async-done | bytes 2752544 | tf_op jit(solution)/shard_map/all_to_all | solution.py:102
  (71 shorter events, 29.0 us)
Async XLA Ops:
  7.2 25.5 %copy-start = (bf16[16,112,128]{2,1,0:T(8,128)(2,1)S(1)}, bf16[16,112,128]{2,1,0:T(8,128)(2,1)}, u32[]{:S(2)}) copy-start(bf16[16,112,128]{2,1,0:T(8,128)(2,1)} %param.19) | copy-start | bytes 1376260
  7.2 25.4 %copy-start.6 = (s32[16]{0:T(128)S(1)}, s32[16]{0:T(128)}, u32[]{:S(2)}) copy-start(s32[16]{0:T(128)} %param.17) | copy-start | bytes 196
  7.2 26.2 %copy-start.1 = (bf16[16,112,128]{2,1,0:T(8,128)(2,1)S(1)}, bf16[16,112,128]{2,1,0:T(8,128)(2,1)}, u32[]{:S(2)}) copy-start(bf16[16,112,128]{2,1,0:T(8,128)(2,1)} %param.18) | copy-start | bytes 1376260
  14.3 20.0 %copy-start.3 = (bf16[128,224]{0,1:T(8,128)(2,1)S(1)}, bf16[128,224]{0,1:T(8,128)(2,1)}, u32[]{:S(2)}) copy-start(bf16[128,224]{0,1:T(8,128)(2,1)} %param.21) | copy-start | bytes 172036
  16.2 32.2 %all-to-all-start = ((bf16[32,8,224]{2,1,0:T(8,128)(2,1)}), bf16[32,8,224]{2,1,0:T(8,128)(2,1)S(1)}, u32[]{:S(2)}, u32[]{:S(2)}) async-start(bf16[32,8,224]{2,1,0:T(8,128)(2,1)} %select_bitcast_fusion.1), calls=%async_computation | async-start | bytes 262144 | tf_op jit(solution)/shard_map/all_to_all | solution.py:52
  48.4 19.7 %all-to-all-start.3 = ((bf16[32,8,224]{2,1,0:T(8,128)(2,1)}), bf16[32,8,224]{2,1,0:T(8,128)(2,1)S(1)}, u32[]{:S(2)}, u32[]{:S(2)}) async-start(bf16[32,8,224]{2,1,0:T(8,128)(2,1)} %fusion.11), calls=%async_computation.4 | async-start | bytes 262144 | tf_op jit(solution)/shard_map/all_to_all | solution.py:52
  68.1 129.4 %all-to-all-start.1 = ((bf16[32,112,384]{2,1,0:T(8,128)(2,1)}), bf16[32,112,384]{2,1,0:T(8,128)(2,1)S(1)}, u32[]{:S(2)}, u32[]{:S(2)}) async-start(bf16[32,112,384]{2,1,0:T(8,128)(2,1)} %pad_maximum_fusion), calls=%async_computation.1 | async-start | bytes 5505024 | tf_op jit(solution)/shard_map/all_to_all | solution.py:36
  73.1 70.8 %all-gather.3.cloned.1.call-start = ((), (), s32[]{:S(2)}) async-start(), calls=%async_computation.8 | async-start | bytes 1949696 | tf_op jit(solution)/shard_map/all_gather | solution.py:55
  73.9 136.8 %all-gather.5.cloned.1.call-start = ((), (), s32[]{:S(2)}) async-start(), calls=%async_computation.10 | async-start | bytes 1949696 | tf_op jit(solution)/shard_map/all_gather | solution.py:55
  74.7 231.8 %reduce-scatter.5.cloned.1.call-start = ((), (), s32[]{:S(2)}) async-start(), calls=%async_computation.11 | async-start | bytes 1949696 | tf_op jit(solution)/shard_map/reduce_scatter | solution.py:58
  214.7 189.4 %reduce-scatter.3.cloned.1.call-start = ((), (), s32[]{:S(2)}) async-start(), calls=%async_computation.9 | async-start | bytes 1949696 | tf_op jit(solution)/shard_map/reduce_scatter | solution.py:58
  308.2 97.5 %all-to-all-start.4 = ((bf16[32,8,224]{2,1,0:T(8,128)(2,1)}), bf16[32,8,224]{2,1,0:T(8,128)(2,1)S(1)}, u32[]{:S(2)}, u32[]{:S(2)}) async-start(bf16[32,8,224]{2,1,0:T(8,128)(2,1)} %bitcast.14), calls=%async_computation.6 | async-start | bytes 262144 | tf_op jit(solution)/shard_map/all_to_all | solution.py:64
  405.7 27.6 %all-to-all-start.2 = ((bf16[32,8,224]{2,1,0:T(8,128)(2,1)}), bf16[32,8,224]{2,1,0:T(8,128)(2,1)S(1)}, u32[]{:S(2)}, u32[]{:S(2)}) async-start(bf16[32,8,224]{2,1,0:T(8,128)(2,1)} %bitcast.9), calls=%async_computation.3 | async-start | bytes 262144 | tf_op jit(solution)/shard_map/all_to_all | solution.py:64
  422.7 16.2 %copy-start.4 = (s32[128,1]{0,1:T(1,128)S(1)}, s32[128,1]{0,1:T(1,128)}, u32[]{:S(2)}) copy-start(s32[128,1]{0,1:T(1,128)} %param.15) | copy-start | bytes 1540
  422.7 20.3 %copy-start.5 = (f32[128,1]{0,1:T(1,128)S(1)}, f32[128,1]{0,1:T(1,128)}, u32[]{:S(2)}) copy-start(f32[128,1]{0,1:T(1,128)} %param.16) | copy-start | bytes 1540
  433.3 0.7 copy-start.2
  434.0 129.1 %all-to-all-start.5 = ((bf16[32,112,384]{2,1,0:T(8,128)(2,1)}), bf16[32,112,384]{2,1,0:T(8,128)(2,1)S(1)}, u32[]{:S(2)}, u32[]{:S(2)}) async-start(bf16[32,112,384]{2,1,0:T(8,128)(2,1)} %pad_maximum_fusion.1), calls=%async_computation.7 | async-start | bytes 5505024 | tf_op jit(solution)/shard_map/all_to_all | solution.py:102
Sparse Core Ops, SparseCore 0:
  77.7 66.0 all-gather.2
  147.7 62.8 all-gather.4
  215.4 91.0 reduce-scatter.4
  311.9 92.1 reduce-scatter.2
where the time goes:
time: 574 us; the launch traced here: 573 us
  waiting for transfers between devices  453 us (79%)
  starting transfers between devices  57.1 us (10%)
  local copies, waits for them, and re-layouts  21.6 us (4%)
  between operations  14.1 us (2%)
  other arithmetic  13.8 us (2%)
  matrix products  13.8 us (2%)
    reduce_scatter x2, waiting for transfers between devices, combine(): lax.psum_scatter(part_rows.astype(jnp.float32).astype(jnp.bfloat16), 'grp...  171 us
    all_to_all x1, waiting for transfers between devices, shards(): lax.all_to_all(slot_grad.reshape(ep_size, stored, 3 * hidden), 'ep', spli...  118 us
    all_gather x2, waiting for transfers between devices, deliver(): lax.all_gather(moved.reshape(pad_rows, -1), 'grp', axis=1, tiled=True)  79.1 us
    all_to_all x1, waiting for transfers between devices, shards(): lax.all_to_all(packed, 'ep', split_axis=0, concat_axis=0, tiled=True)  53.7 us
    all_to_all x2, starting transfers between devices, combine(): lax.all_to_all(block_sum.reshape(ep_size, capacity, -1).astype(jnp.bfloat...  26 us
    all_to_all x2, starting transfers between devices, deliver(): lax.all_to_all(send_rows.reshape(ep_size, capacity, -1), 'ep', split_axis...  21.1 us
    all_to_all x2, waiting for transfers between devices, deliver(): lax.all_to_all(send_rows.reshape(ep_size, capacity, -1), 'ep', split_axis...  20.2 us
  transfers between devices with their start and end apart: 10, of which 9 were waited for; matrix products, arithmetic and copies ran while one was open for 6% of the time, Pallas kernels for 0%

commit v1 on v0

v1 whole, which is shorter than its diff:
```python
import functools

import jax
import jax.numpy as jnp
from jax import lax
from jax.experimental import pallas as pl
from jax.experimental.pallas import tpu as pltpu
from jax.sharding import PartitionSpec as P

MESH = pl.DeviceIdType.MESH
BF = jnp.bfloat16
F32 = jnp.float32
NX, NY, NZ, NEP, NGRP = 4, 2, 16, 32, 16
LAST = (((1,), (1,)), ((), ()))
FIRST = (((0,), (0,)), ((), ()))


def mm(a, b, dims=(((1,), (0,)), ((), ()))):
    return lax.dot_general(a, b, dims, preferred_element_type=F32)


def body(
    tok_ref, routes_ref, rw_ref, hot_ref, wg_ref, wu_ref, wd_ref, cot_ref,
    out_ref, gtok_ref, gg_ref, gu_ref, gd_ref,
    src, meta, a1r, xb, er, et, wall, xe, se, pa, pb, ya, ra, rb, yb,
    ha, hb, he, qq, rc, rfar, rx, ry, fin, b1r, b2r, tot, go,
    w_sem, o_sem, a1_s, a1_q, m_s, m_q, a2_s, a2_q, g3_s, g3_q,
    ya_s, ya_q, ra_s, ra_q, rb_s, rb_q, yb_s, yb_q,
    hy_s, hy_q, ga_s, ga_q, gb_s, gb_q, gy_s, gy_q,
    c5_s, c5_q, f5_s, f5_q, x5_s, x5_q, y5_s, y5_q, b1_s, b1_q, b2_s, b2_q,
):
    g = lax.axis_index("grp")
    p = lax.axis_index("ep")
    x, yh, c = g // 4, (g // 2) % 2, g % 2
    y, z = p // NZ, p % NZ
    zr, zl = y * NZ + (z + 1) % NZ, y * NZ + (z + NZ - 1) % NZ
    py = (1 - y) * NZ + z
    gi = lambda xx, hh, cc: xx * 4 + hh * 2 + cc
    xr, xl = (x + 1) % NX, (x + 3) % NX
    gr, gl = gi(xr, yh, c), gi(xl, yh, c)
    gy, gc = gi(x, 1 - yh, c), gi(x, yh, 1 - c)

    def put(s, d, ss, rs, **dev):
        return pltpu.make_async_remote_copy(
            src_ref=s, dst_ref=d, send_sem=ss, recv_sem=rs, device_id=dev, device_id_type=MESH
        )

    w_in = [
        pltpu.make_async_copy(r, wall.at[:, pl.ds(0, 112), pl.ds(128 * i, 128)], w_sem.at[i])
        for i, r in enumerate((wg_ref, wu_ref, wd_ref))
    ]
    for cp in w_in:
        cp.start()

    barrier = pltpu.get_barrier_semaphore()

    def hello_g(i, _):
        pl.semaphore_signal(barrier, inc=1, device_id={"grp": (g + i) % NGRP}, device_id_type=MESH)
        return 0

    def hello_e(i, _):
        pl.semaphore_signal(barrier, inc=1, device_id={"ep": (p + i) % NEP}, device_id_type=MESH)
        return 0

    lax.fori_loop(1, NGRP, hello_g, 0)
    lax.fori_loop(1, NEP, hello_e, 0)

    slot_row = routes_ref[...]
    rw_row = rw_ref[...]
    dz = (cot_ref[...].astype(F32) * rw_row).astype(BF)
    for h in range(2):
        src[0:7, h] = tok_ref[h * 112 : (h + 1) * 112, :].reshape(7, 16, 128)
        src[8:15, h] = dz[h * 112 : (h + 1) * 112, :].reshape(7, 16, 128)
    src[7] = jnp.zeros((2, 16, 128), BF)
    src[15] = jnp.zeros((2, 16, 128), BF)
    wall[:, 112:128, :] = jnp.zeros((16, 16, 384), BF)

    oh = jnp.where(lax.broadcasted_iota(jnp.int32, (NEP, 128), 0) == slot_row, 1.0, 0.0).astype(F32)
    upper = jnp.where(
        lax.broadcasted_iota(jnp.int32, (128, 128), 0) < lax.broadcasted_iota(jnp.int32, (128, 128), 1), 1.0, 0.0
    ).astype(BF)
    before = mm(oh.astype(BF), upper)
    pos_row = jnp.sum(oh * before, axis=0, keepdims=True)
    row_id = lax.broadcasted_iota(jnp.int32, (16, 128), 0)
    mrows = jnp.where(row_id == 0, slot_row.astype(F32), jnp.where(row_id == 1, pos_row, 0.0))
    meta[p] = mrows.astype(BF)

    pl.semaphore_wait(barrier, NGRP + NEP - 2)

    a1 = lambda i, t: put(src.at[t], a1r.at[g], a1_s.at[i], a1_q.at[i], grp=t)
    mt = lambda i, t: put(meta.at[p], meta.at[p], m_s.at[i], m_q.at[i], ep=t)
    a2 = lambda i, t: put(a1r.at[t // 2, t % 2], xb.at[g, p], a2_s.at[i], a2_q.at[i], ep=t)

    def loop(lo, hi, f):
        def step(i, _):
            f(i)
            return 0

        lax.fori_loop(lo, hi, step, 0)

    loop(1, NGRP, lambda i: a1(i, (g + i) % NGRP).start())
    loop(1, NEP, lambda i: mt(i, (p + i) % NEP).start())
    a1r[g] = src[g]

    def a1_wait(i):
        f = (g + NGRP - i) % NGRP
        put(src.at[f], a1r.at[f], a1_s.at[i], a1_q.at[i], grp=f).wait_recv()

    loop(1, NGRP, a1_wait)
    loop(1, NEP, lambda i: a2(i, (p + i) % NEP).start())
    xb[g, p] = a1r[p // 2, p % 2]

    def m_wait(i):
        f = (p + NEP - i) % NEP
        put(meta.at[p], meta.at[f], m_s.at[i], m_q.at[i], ep=f).wait_recv()

    loop(1, NEP, m_wait)

    def build(q):
        m0 = meta[2 * q].astype(F32)
        m1 = meta[2 * q + 1].astype(F32)
        d0 = m0[0:1, :] * 16.0 + m0[1:2, :]
        d1 = m1[0:1, :] * 16.0 + m1[1:2, :] + 8.0
        row = jnp.concatenate([d0, d1], axis=1)
        irow = row.astype(jnp.int32)
        er[q] = jnp.where(
            lax.broadcasted_iota(jnp.int32, (512, 256), 0) == irow, 1.0, 0.0
        ).astype(BF)
        col = jnp.transpose(jnp.broadcast_to(row, (128, 256))).astype(jnp.int32)
        for b in range(4):
            et[q, :, 128 * b : 128 * (b + 1)] = jnp.where(
                lax.broadcasted_iota(jnp.int32, (256, 128), 1) + 128 * b == col, 1.0, 0.0
            ).astype(BF)

    def a2_wait(i):
        f = (p + NEP - i) % NEP
        put(a1r.at[0, 0], xb.at[g, f], a2_s.at[i], a2_q.at[i], ep=f).wait_recv()

    loop(0, 4, build)
    loop(1, NEP, a2_wait)

    def g3(chunk, i, t):
        return put(xb.at[chunk], xb.at[chunk], g3_s.at[i], g3_q.at[i], grp=t)

    g3(g, 0, gy).start()
    g3(g, 1 + yh, gr).start()
    g3(g, 3 + yh, gl).start()
    g3(g, 7 + yh, gc).start()
    loop(4, 8, build)
    g3(gy, 0, gy).wait_recv()
    g3(gy, 1 + (1 - yh), gr).start()
    g3(gy, 3 + (1 - yh), gl).start()
    g3(gy, 7 + (1 - yh), gc).start()
    loop(8, 12, build)
    xf = (x + 2) % NX
    g3(gi(xl, 0, c), 1, gr).wait_recv()
    g3(gi(xl, 0, c), 5, gr).start()
    g3(gi(xl, 0, c), 7 + 6, gc).start()
    g3(gi(xr, 1, c), 4, gl).wait_recv()
    g3(gi(xr, 1, c), 6, gl).start()
    g3(gi(xr, 1, c), 7 + 3, gc).start()
    g3(gi(xl, 1, c), 2, gr).wait_recv()
    g3(gi(xl, 1, c), 7 + 7, gc).start()
    g3(gi(xr, 0, c), 3, gl).wait_recv()
    g3(gi(xr, 0, c), 7 + 2, gc).start()
    loop(12, 16, build)
    for h in range(2):
        g3(gi(xf, h, c), 5 + h, gr).wait_recv()
        g3(gi(xf, h, c), 7 + 4 + h, gc).start()
    for dx in range(4):
        for h in range(2):
            g3(gi((x + dx) % NX, h, 1 - c), 7 + 2 * dx + h, gc).wait_recv()

    for cp in w_in:
        cp.wait()

    def spread(q):
        t0 = xb[:, 2 * q].reshape(256, 128)
        t1 = xb[:, 2 * q + 1].reshape(256, 128)
        xe[q] = mm(er[q], jnp.concatenate([t0, t1], axis=1), LAST).astype(BF)

    loop(0, 16, spread)

    def host(s):
        return jnp.where(s < 16, s, hot_ref[jnp.maximum(s - 16, 0)])

    def first_dots(s):
        w = wall[host(s)]
        rows = pl.ds(pl.multiple_of(s * 16, 16), 16)
        xd = xe[:, rows, :].reshape(256, 256)
        se[:, rows, 0:256] = mm(xd[:, 0:128], w[:, 0:256]).astype(BF).reshape(16, 16, 256)
        se[:, rows, 256:384] = mm(xd[:, 128:256], w[:, 256:384]).astype(BF).reshape(16, 16, 128)

    loop(0, 32, first_dots)

    def squeeze(q):
        cc = mm(et[q], se[q]).astype(BF)
        zp = q % 8
        pa[pl.ds(2 * q, 2)] = cc[:, 0:256].reshape(2, 128, 256)
        for i in range(2):
            pb[2 * zp + i, q // 8] = cc[128 * i : 128 * (i + 1), 256:384]

    def ya_put(t):
        return put(pa.at[(1 - y) * NZ + t], ya.at[t], ya_s.at[t], ya_q.at[t], ep=py)

    def near(i):
        off = jnp.where(i % 2 == 1, 4 - (i + 1) // 2, 4 + i // 2)
        return (z // 2 + off) % 8

    def squeeze_far(i):
        zp = near(i)
        squeeze((1 - y) * 8 + zp)
        ya_put(2 * zp).start()
        ya_put(2 * zp + 1).start()

    loop(0, 8, squeeze_far)
    loop(0, 8, lambda i: squeeze(y * 8 + near(i)))

    def target(d, n, k):
        return (z + NZ + (n - k if d == 0 else k - n)) % NZ

    def a_step(d, n, k):
        t = target(d, n, k)
        ya_put(t).wait_recv()
        v = pa[y * NZ + t].astype(F32) + ya[t].astype(F32)
        if not (isinstance(k, int) and k == 0):
            put(pa.at[0], ra.at[d, k - 1], ra_s.at[d, k - 1], ra_q.at[d, k - 1], ep=zr).wait_recv()
            v = v + ra[d, k - 1].astype(F32)
        pa[y * NZ + t] = v.astype(BF)
        put(
            pa.at[y * NZ + t], ra.at[d, k], ra_s.at[d, k], ra_q.at[d, k], ep=zr if d == 0 else zl
        ).start()

    def b_step(d, n, k):
        t = target(d, n, k)
        if not (isinstance(k, int) and k == 0):
            put(pb.at[0], rb.at[d, k - 1], rb_s.at[d, k - 1], rb_q.at[d, k - 1], ep=zr).wait_recv()
            pb[t] = (pb[t].astype(F32) + rb[d, k - 1].astype(F32)).astype(BF)
        put(pb.at[t], rb.at[d, k], rb_s.at[d, k], rb_q.at[d, k], ep=zr if d == 0 else zl).start()

    def all_steps(k):
        b_step(0, 7, k)
        b_step(1, 8, k)
        a_step(0, 8, k)
        a_step(1, 7, k)

    all_steps(0)
    loop(1, 7, all_steps)
    b_step(1, 8, 7)
    a_step(0, 8, 7)
    put(pb.at[0], rb.at[0, 6], rb_s.at[0, 6], rb_q.at[0, 6], ep=zr).wait_recv()
    put(pb.at[0], rb.at[1, 7], rb_s.at[1, 7], rb_q.at[1, 7], ep=zr).wait_recv()
    ag_own = (
        pb[z, y].astype(F32) + rb[0, 6, y].astype(F32) + rb[1, 7, y].astype(F32)
    )
    pb[z, 1 - y] = (
        pb[z, 1 - y].astype(F32) + rb[0, 6, 1 - y].astype(F32) + rb[1, 7, 1 - y].astype(F32)
    ).astype(BF)
    yb_put = put(pb.at[z, 1 - y], yb, yb_s, yb_q, ep=py)
    yb_put.start()
    ya_put(z).wait_recv()
    put(pa.at[0], ra.at[1, 6], ra_s.at[1, 6], ra_q.at[1, 6], ep=zr).wait_recv()
    put(pa.at[0], ra.at[0, 7], ra_s.at[0, 7], ra_q.at[0, 7], ep=zr).wait_recv()
    pre = (
        pa[p].astype(F32) + ya[z].astype(F32) + ra[0, 7].astype(F32) + ra[1, 6].astype(F32)
    )
    gate, up = pre[:, 0:128], pre[:, 128:256]
    sg = jax.nn.sigmoid(gate)
    hb[z, y] = (gate * sg * up).astype(BF)
    hy_put = put(hb.at[z, y], hb.at[z, y], hy_s, hy_q, ep=py)
    hy_put.start()
    yb_put.wait_recv()
    ag = ag_own + yb[...].astype(F32)
    ha[p, :, 0:128] = (ag * up * sg * (1.0 + gate * (1.0 - sg))).astype(BF)
    ha[p, :, 128:256] = (ag * gate * sg).astype(BF)

    def origin(d, k):
        return (z + NZ + (-k if d == 0 else k)) % NZ

    def ga_put(d, k, o):
        return put(
            ha.at[y * NZ + o], ha.at[y * NZ + o], ga_s.at[d, k], ga_q.at[d, k], ep=zr if d == 0 else zl
        )

    def gb_put(d, k, o):
        return put(hb.at[o], hb.at[o], gb_s.at[d, k], gb_q.at[d, k], ep=zr if d == 0 else zl)

    def gy_put(yy, o):
        return put(ha.at[yy * NZ + o], ha.at[yy * NZ + o], gy_s.at[o], gy_q.at[o], ep=py)

    ga_put(0, 0, z).start()
    ga_put(1, 0, z).start()
    gy_put(y, z).start()
    put(hb.at[z, 1 - y], hb.at[z, 1 - y], hy_s, hy_q, ep=py).wait_recv()
    gb_put(0, 0, z).start()
    gb_put(1, 0, z).start()

    def ga_step(d, k, more=True):
        o = origin(d, k)
        ga_put(d, k - 1, o).wait_recv()
        if more:
            ga_put(d, k, o).start()
        gy_put(y, o).start()

    def gb_step(d, k, more=True):
        o = origin(d, k)
        gb_put(d, k - 1, o).wait_recv()
        if more:
            gb_put(d, k, o).start()

    def gather_steps(k):
        ga_step(0, k)
        ga_step(1, k)
        gb_step(0, k)
        gb_step(1, k)

    loop(1, 7, gather_steps)
    ga_step(0, 7)
    ga_step(1, 7, False)
    gb_step(0, 7, False)
    gb_step(1, 7)
    ga_step(0, 8, False)
    gb_step(1, 8, False)

    def spread_back(q):
        zp = q % 8
        hq = jnp.concatenate(
            [
                ha[pl.ds(2 * q, 2)].reshape(256, 256),
                jnp.concatenate([hb[2 * zp, q // 8], hb[2 * zp + 1, q // 8]], axis=0),
            ],
            axis=1,
        )
        he[q] = mm(er[q], hq).astype(BF)

    loop(0, 8, lambda i: spread_back(y * 8 + i))
    loop(0, 16, lambda o: gy_put(1 - y, o).wait_recv())
    loop(0, 8, lambda i: spread_back((1 - y) * 8 + i))

    def back_dots(s):
        w = wall[host(s)]
        rows = pl.ds(pl.multiple_of(s * 16, 16), 16)
        hs = he[:, rows, :].reshape(256, 384)
        se[:, rows, 0:128] = mm(hs[:, 256:384], w[:, 256:384], LAST).astype(BF).reshape(16, 16, 128)
        se[:, rows, 128:256] = mm(hs[:, 0:256], w[:, 0:256], LAST).astype(BF).reshape(16, 16, 128)

    loop(0, 32, back_dots)

    def squeeze_out(q):
        cc = mm(et[q], se[q, :, 0:256]).astype(BF)
        for i in range(2):
            for kind in range(2):
                qq[kind * 8 : (kind + 1) * 8, 2 * q + i] = cc[
                    128 * i : 128 * (i + 1), 128 * kind : 128 * (kind + 1)
                ].reshape(8, 16, 128)

    loop(0, 16, squeeze_out)

    def c5(dx, h):
        i = 2 * dx + h
        return put(qq.at[gi((x + dx) % NX, h, 1 - c)], rc.at[i], c5_s.at[i], c5_q.at[i], grp=gc)

    order = (2, 1, 3, 0)
    for dx in order:
        for h in range(2):
            c5(dx, h).start()

    def weight_dots(s):
        rows = pl.ds(pl.multiple_of(s * 16, 16), 16)
        xd = xe[:, rows, :].reshape(256, 256)
        hs = he[:, rows, :].reshape(256, 384)
        tot[s, :, 0:256] = mm(xd[:, 0:128], hs[:, 0:256], FIRST)[0:112].astype(BF).astype(F32)
        tot[s, :, 256:384] = mm(xd[:, 128:256], hs[:, 256:384], FIRST)[0:112].astype(BF).astype(F32)

    def addto(t, r):
        qq[t] = (qq[t].astype(F32) + r.astype(F32)).astype(BF)

    def with_core(dx, h):
        c5(dx, h).wait_recv()
        addto(gi((x + dx) % NX, h, c), rc[2 * dx + h])

    def f5(h):
        return put(qq.at[gi(xf, h, c)], rfar.at[h], f5_s.at[h], f5_q.at[h], grp=gr if h == 0 else gl)

    def x5(d, h):
        t = xr if d == 0 else xl
        return put(
            qq.at[gi(t, h, c)], rx.at[d, h], x5_s.at[d, h], x5_q.at[d, h], grp=gr if d == 0 else gl
        )

    loop(0, 4, weight_dots)
    for h in range(2):
        with_core(2, h)
        f5(h).start()
    with_core(1, 1)
    x5(0, 1).start()
    with_core(3, 0)
    x5(1, 0).start()
    with_core(1, 0)
    with_core(3, 1)
    f5(0).wait_recv()
    addto(gi(xr, 0, c), rfar[0])
    x5(0, 0).start()
    f5(1).wait_recv()
    addto(gi(xl, 1, c), rfar[1])
    x5(1, 1).start()
    loop(4, 12, weight_dots)
    for h in range(2):
        c5(0, h).wait_recv()
        for d in range(2):
            x5(d, h).wait_recv()

    def own_sum(h):
        return (
            qq[gi(x, h, c)].astype(F32)
            + rc[h].astype(F32)
            + rx[0, h].astype(F32)
            + rx[1, h].astype(F32)
        )

    qq[gy] = own_sum(1 - yh).astype(BF)
    y5 = put(qq.at[gy], ry, y5_s, y5_q, grp=gy)
    y5.start()
    loop(12, 20, weight_dots)
    mine = own_sum(yh)
    y5.wait_recv()
    fin[...] = (mine + ry[...].astype(F32)).astype(BF)

    b1 = lambda i, t: put(fin.at[t], b1r.at[p // 2, p % 2], b1_s.at[i], b1_q.at[i], ep=t)
    b2 = lambda i, t: put(b1r.at[t], b2r.at[g], b2_s.at[i], b2_q.at[i], grp=t)
    loop(1, NEP, lambda i: b1(i, (p + i) % NEP).start())
    b1r[p // 2, p % 2] = fin[p]
    loop(20, 32, weight_dots)

    def b1_wait(i):
        f = (p + NEP - i) % NEP
        put(fin.at[0], b1r.at[f // 2, f % 2], b1_s.at[i], b1_q.at[i], ep=f).wait_recv()

    loop(1, NEP, b1_wait)
    loop(1, NGRP, lambda i: b2(i, (g + i) % NGRP).start())
    b2r[g] = b1r[g]

    def chain(j):
        e = hot_ref[j]

        def look(i, prev):
            return jnp.where((i < j) & (hot_ref[i] == e), 16 + i, prev)

        prev = lax.fori_loop(0, 16, look, e)
        tot[16 + j] = tot[16 + j] + tot[prev]

    loop(0, 16, chain)

    def close(e):
        last = lax.fori_loop(0, 16, lambda i, v: jnp.where(hot_ref[i] == e, 16 + i, v), e)
        v = tot[last].astype(BF)
        for i in range(3):
            go[i, e] = v[:, 128 * i : 128 * (i + 1)]

    loop(0, 16, close)
    w_out = [
        pltpu.make_async_copy(go.at[i], r, o_sem.at[i]) for i, r in enumerate((gg_ref, gu_ref, gd_ref))
    ]
    for cp in w_out:
        cp.start()

    def b2_wait(i):
        f = (g + NGRP - i) % NGRP
        put(b1r.at[0], b2r.at[f], b2_s.at[i], b2_q.at[i], grp=f).wait_recv()

    loop(1, NGRP, b2_wait)
    for kind, ref in enumerate((out_ref, gtok_ref)):
        for h in range(2):
            rows = b2r[kind * 8 : (kind + 1) * 8, h].reshape(128, 128).astype(F32)
            v = jnp.transpose(rows)[0:112]
            if kind == 0:
                v = v * rw_row
            ref[h * 112 : (h + 1) * 112, :] = v.astype(BF)

    loop(1, NGRP, lambda i: a1(i, (g + i) % NGRP).wait_send())
    loop(1, NEP, lambda i: mt(i, (p + i) % NEP).wait_send())
    loop(1, NEP, lambda i: a2(i, (p + i) % NEP).wait_send())
    loop(0, 15, lambda i: g3(g, i, gy).wait_send())
    loop(0, 16, lambda t: ya_put(t).wait_send())
    for d in range(2):
        na, nb = (8, 7) if d == 0 else (7, 8)
        loop(0, na, lambda k: put(pa.at[0], ra.at[d, k], ra_s.at[d, k], ra_q.at[d, k], ep=zr).wait_send())
        loop(0, nb, lambda k: put(pb.at[0], rb.at[d, k], rb_s.at[d, k], rb_q.at[d, k], ep=zr).wait_send())
        loop(0, na, lambda k: ga_put(d, k, z).wait_send())
        loop(0, nb, lambda k: gb_put(d, k, z).wait_send())
    yb_put.wait_send()
    hy_put.wait_send()
    loop(0, 16, lambda o: gy_put(y, o).wait_send())
    for dx in range(4):
        for h in range(2):
            c5(dx, h).wait_send()
    for h in range(2):
        f5(h).wait_send()
        for d in range(2):
            x5(d, h).wait_send()
    y5.wait_send()
    loop(1, NEP, lambda i: b1(i, (p + i) % NEP).wait_send())
    loop(1, NGRP, lambda i: b2(i, (g + i) % NGRP).wait_send())
    for cp in w_out:
        cp.wait()


def layer(tokens, routes, route_weights, hot_experts, w_gate, w_up, w_down, cotangent):
    v = pltpu.VMEM
    dma = pltpu.SemaphoreType.DMA
    vm = pl.BlockSpec(memory_space=pltpu.VMEM)
    anym = pl.BlockSpec(memory_space=pl.ANY)
    sems = [
        (3,), (3,), (16,), (16,), (32,), (32,), (32,), (32,), (15,), (15,),
        (16,), (16,), (2, 8), (2, 8), (2, 8), (2, 8), None, None,
        None, None, (2, 8), (2, 8), (2, 8), (2, 8), (16,), (16,),
        (8,), (8,), (2,), (2,), (2, 2), (2, 2), None, None, (32,), (32,), (16,), (16,),
    ]
    out_t, gtok_t, gg, gu, gd = pl.pallas_call(
        body,
        out_shape=(
            jax.ShapeDtypeStruct((224, 128), BF),
            jax.ShapeDtypeStruct((224, 128), BF),
            jax.ShapeDtypeStruct((16, 112, 128), BF),
            jax.ShapeDtypeStruct((16, 112, 128), BF),
            jax.ShapeDtypeStruct((16, 112, 128), BF),
        ),
        in_specs=[vm, vm, vm, pl.BlockSpec(memory_space=pltpu.SMEM), anym, anym, anym, vm],
        out_specs=(vm, vm, anym, anym, anym),
        scratch_shapes=[
            v((16, 2, 16, 128), BF),
            v((32, 16, 128), BF),
            v((16, 2, 16, 128), BF),
            v((16, 32, 16, 128), BF),
            v((16, 512, 256), BF),
            v((16, 256, 512), BF),
            v((16, 128, 384), BF),
            v((16, 512, 256), BF),
            v((16, 512, 384), BF),
            v((32, 128, 256), BF),
            v((16, 2, 128, 128), BF),
            v((16, 128, 256), BF),
            v((2, 8, 128, 256), BF),
            v((2, 8, 2, 128, 128), BF),
            v((128, 128), BF),
            v((32, 128, 256), BF),
            v((16, 2, 128, 128), BF),
            v((16, 512, 384), BF),
            v((16, 32, 16, 128), BF),
            v((8, 32, 16, 128), BF),
            v((2, 32, 16, 128), BF),
            v((2, 2, 32, 16, 128), BF),
            v((32, 16, 128), BF),
            v((32, 16, 128), BF),
            v((16, 2, 16, 128), BF),
            v((16, 2, 16, 128), BF),
            v((32, 112, 384), F32),
            v((3, 16, 112, 128), BF),
        ]
        + [dma if s is None else dma(s) for s in sems],
        compiler_params=pltpu.CompilerParams(
            collective_id=0, has_side_effects=True, vmem_limit_bytes=60 * 1024 * 1024
        ),
        cost_estimate=pl.CostEstimate(flops=8 * 10**9, bytes_accessed=3 * 10**6, transcendentals=0),
    )(
        tokens.T,
        routes.reshape(1, 128),
        route_weights.reshape(1, 128),
        hot_experts,
        w_gate,
        w_up,
        jnp.swapaxes(w_down, 1, 2),
        cotangent.T,
    )
    return out_t.T, gtok_t.T, gg, gu, jnp.swapaxes(gd, 1, 2)


def solution(mesh):
    placed = (
        P("ep", "grp"),
        P("ep", None),
        P("ep", None),
        P(),
        P(None, "ep", "grp"),
        P(None, "ep", "grp"),
        P(None, "grp", "ep"),
        P("ep", "grp"),
    )
    return jax.shard_map(
        layer,
        mesh=mesh,
        in_specs=placed,
        out_specs=(
            P("ep", "grp"),
            P("ep", "grp"),
            P(None, "ep", "grp"),
            P(None, "ep", "grp"),
            P(None, "grp", "ep"),
        ),
        check_vma=False,
    )
```

time: 574 us -> 194 us (0.34)
  the two profiles are of different devices: /device:TPU:32 before, /device:TPU:1 now
where the time goes in v1:
time: 194 us
  Pallas kernels  187 us (96%)
  local copies, waits for them, and re-layouts  5.91 us (3%)
    pallas_call x1, Pallas kernels, layer(): pl.pallas_call(body, out_shape=(jax.ShapeDtypeStruct((224, 128), BF), jax...  187 us
    unnamed x11, local copies, waits for them, and re-layouts  5.91 us

profile of v1, /device:TPU:1, one launch (start us, length us, event | category | flops | bytes accessed | tf_op | source)
XLA Modules:
  0.0 193.7 jit_solution(15846849342004844530)
XLA Ops:
  0.6 187.2 %shard_map.119 = (bf16[224,128]{1,0:T(8,128)(2,1)}, bf16[224,128]{1,0:T(8,128)(2,1)}, bf16[16,112,128]{2,1,0:T(8,128)(2,1)}, bf16[16,112,128]{2,1,0:T(8,128)(2,1)}, bf16[16,112,128]{2,1,0:T(8,128)(2,1)}) custom-call(bf16[224,128]{1,0:T(8,128)(2,1)} %bitcast.12, s32[1,128]{1,0:T(1,128)} %bitcast.14, f32[1,128]{1,0:T(1,128)} %bitcast.15, s32[16]{0:T(128)} %hot_ref.1, ...), custom_call_target="tpu_custom_call" | custom-call | flops 8000000000 | bytes 3000000 | tf_op jit(solution)/shard_map/pallas_call | solution.py:519
  187.8 0.0 copy-start.2
  187.8 1.5 copy.18
  189.3 0.0 copy-done.2
  189.3 0.6 copy.19
  189.9 0.0 copy-start.1
  189.9 1.9 copy.20
  191.8 0.0 copy-done.1
  191.8 0.0 copy-start
  191.8 0.8 copy.21
  192.6 0.4 copy-done
  193.0 0.8 copy.22
Async XLA Ops:
  187.8 1.5 copy-start.2
  189.9 1.9 copy-start.1
  191.8 1.2 copy-start

commit v2 on v1

--- a/solution.py
+++ b/solution.py
@@ -21,13 +21,13 @@
 
 def body(
     tok_ref, routes_ref, rw_ref, hot_ref, wg_ref, wu_ref, wd_ref, cot_ref,
-    out_ref, gtok_ref, gg_ref, gu_ref, gd_ref,
+    rows_ref, slots_ref,
     src, meta, a1r, xb, er, et, wall, xe, se, pa, pb, ya, ra, rb, yb,
-    ha, hb, he, qq, rc, rfar, rx, ry, fin, b1r, b2r, tot, go,
+    ha, hb, he, qq, rc, rfar, rx, ry, fin, b2r, tot,
     w_sem, o_sem, a1_s, a1_q, m_s, m_q, a2_s, a2_q, g3_s, g3_q,
     ya_s, ya_q, ra_s, ra_q, rb_s, rb_q, yb_s, yb_q,
     hy_s, hy_q, ga_s, ga_q, gb_s, gb_q, gy_s, gy_q,
-    c5_s, c5_q, f5_s, f5_q, x5_s, x5_q, y5_s, y5_q, b1_s, b1_q, b2_s, b2_q,
+    c5_s, c5_q, f5_s, f5_q, x5_s, x5_q, y5_s, y5_q, b1_s, b1_q,
 ):
     g = lax.axis_index("grp")
     p = lax.axis_index("ep")
@@ -52,6 +52,8 @@
     for cp in w_in:
         cp.start()
 
+    tail = []
+
     barrier = pltpu.get_barrier_semaphore()
 
     def hello_g(i, _):
@@ -65,9 +67,19 @@
     lax.fori_loop(1, NGRP, hello_g, 0)
     lax.fori_loop(1, NEP, hello_e, 0)
 
+    def hello_b(i, _):
+        t, h = i // 2, i % 2
+
+        @pl.when(jnp.logical_not((t == g) & (2 * g + h == p)))
+        def _():
+            pl.semaphore_signal(barrier, inc=1, device_id={"grp": t, "ep": 2 * g + h}, device_id_type=MESH)
+
+        return 0
+
+    lax.fori_loop(0, NEP, hello_b, 0)
+
     slot_row = routes_ref[...]
-    rw_row = rw_ref[...]
-    dz = (cot_ref[...].astype(F32) * rw_row).astype(BF)
+    dz = (cot_ref[...].astype(F32) * rw_ref[...]).astype(BF)
     for h in range(2):
         src[0:7, h] = tok_ref[h * 112 : (h + 1) * 112, :].reshape(7, 16, 128)
         src[8:15, h] = dz[h * 112 : (h + 1) * 112, :].reshape(7, 16, 128)
@@ -85,7 +97,7 @@
     mrows = jnp.where(row_id == 0, slot_row.astype(F32), jnp.where(row_id == 1, pos_row, 0.0))
     meta[p] = mrows.astype(BF)
 
-    pl.semaphore_wait(barrier, NGRP + NEP - 2)
+    pl.semaphore_wait(barrier, NGRP + NEP - 2 + NEP - jnp.where(p // 2 == g, 1, 0))
 
     a1 = lambda i, t: put(src.at[t], a1r.at[g], a1_s.at[i], a1_q.at[i], grp=t)
     mt = lambda i, t: put(meta.at[p], meta.at[p], m_s.at[i], m_q.at[i], ep=t)
@@ -98,6 +110,13 @@
 
         lax.fori_loop(lo, hi, step, 0)
 
+    def dots(lo, hi, f, unroll=1):
+        def step(i, _):
+            f(i)
+            return 0
+
+        lax.fori_loop(lo, hi, step, 0, unroll=unroll)
+
     loop(1, NGRP, lambda i: a1(i, (g + i) % NGRP).start())
     loop(1, NEP, lambda i: mt(i, (p + i) % NEP).start())
     a1r[g] = src[g]
@@ -108,6 +127,9 @@
 
     loop(1, NGRP, a1_wait)
     loop(1, NEP, lambda i: a2(i, (p + i) % NEP).start())
+    tail.append(lambda: loop(1, NGRP, lambda i: a1(i, (g + i) % NGRP).wait_send()))
+    tail.append(lambda: loop(1, NEP, lambda i: mt(i, (p + i) % NEP).wait_send()))
+    tail.append(lambda: loop(1, NEP, lambda i: a2(i, (p + i) % NEP).wait_send()))
     xb[g, p] = a1r[p // 2, p % 2]
 
     def m_wait(i):
@@ -136,7 +158,7 @@
         f = (p + NEP - i) % NEP
         put(a1r.at[0, 0], xb.at[g, f], a2_s.at[i], a2_q.at[i], ep=f).wait_recv()
 
-    loop(0, 4, build)
+    dots(0, 4, build)
     loop(1, NEP, a2_wait)
 
     def g3(chunk, i, t):
@@ -146,12 +168,12 @@
     g3(g, 1 + yh, gr).start()
     g3(g, 3 + yh, gl).start()
     g3(g, 7 + yh, gc).start()
-    loop(4, 8, build)
+    dots(4, 8, build)
     g3(gy, 0, gy).wait_recv()
     g3(gy, 1 + (1 - yh), gr).start()
     g3(gy, 3 + (1 - yh), gl).start()
     g3(gy, 7 + (1 - yh), gc).start()
-    loop(8, 12, build)
+    dots(8, 12, build)
     xf = (x + 2) % NX
     g3(gi(xl, 0, c), 1, gr).wait_recv()
     g3(gi(xl, 0, c), 5, gr).start()
@@ -163,7 +185,7 @@
     g3(gi(xl, 1, c), 7 + 7, gc).start()
     g3(gi(xr, 0, c), 3, gl).wait_recv()
     g3(gi(xr, 0, c), 7 + 2, gc).start()
-    loop(12, 16, build)
+    dots(12, 16, build)
     for h in range(2):
         g3(gi(xf, h, c), 5 + h, gr).wait_recv()
         g3(gi(xf, h, c), 7 + 4 + h, gc).start()
@@ -171,6 +193,7 @@
         for h in range(2):
             g3(gi((x + dx) % NX, h, 1 - c), 7 + 2 * dx + h, gc).wait_recv()
 
+    tail.append(lambda: loop(0, 15, lambda i: g3(g, i, gy).wait_send()))
     for cp in w_in:
         cp.wait()
 
@@ -179,7 +202,7 @@
         t1 = xb[:, 2 * q + 1].reshape(256, 128)
         xe[q] = mm(er[q], jnp.concatenate([t0, t1], axis=1), LAST).astype(BF)
 
-    loop(0, 16, spread)
+    dots(0, 16, spread)
 
     def host(s):
         return jnp.where(s < 16, s, hot_ref[jnp.maximum(s - 16, 0)])
@@ -191,7 +214,7 @@
         se[:, rows, 0:256] = mm(xd[:, 0:128], w[:, 0:256]).astype(BF).reshape(16, 16, 256)
         se[:, rows, 256:384] = mm(xd[:, 128:256], w[:, 256:384]).astype(BF).reshape(16, 16, 128)
 
-    loop(0, 32, first_dots)
+    dots(0, 32, first_dots, 1)
 
     def squeeze(q):
         cc = mm(et[q], se[q]).astype(BF)
@@ -213,43 +236,60 @@
         ya_put(2 * zp).start()
         ya_put(2 * zp + 1).start()
 
-    loop(0, 8, squeeze_far)
-    loop(0, 8, lambda i: squeeze(y * 8 + near(i)))
+    dots(0, 8, squeeze_far)
+    dots(0, 8, lambda i: squeeze(y * 8 + near(i)))
+    tail.append(lambda: loop(0, 16, lambda t: ya_put(t).wait_send()))
 
     def target(d, n, k):
         return (z + NZ + (n - k if d == 0 else k - n)) % NZ
 
-    def a_step(d, n, k):
+    def a_put(d, k, t, j):
+        r = pl.ds(64 * j, 64)
+        return put(
+            pa.at[y * NZ + t, r], ra.at[d, k, r], ra_s.at[d, k, j], ra_q.at[d, k, j], ep=zr if d == 0 else zl
+        )
+
+    def b_put(d, k, t, j):
+        return put(
+            pb.at[t, j], rb.at[d, k, j], rb_s.at[d, k, j], rb_q.at[d, k, j], ep=zr if d == 0 else zl
+        )
+
+    def a_step(d, n, k, j):
         t = target(d, n, k)
-        ya_put(t).wait_recv()
-        v = pa[y * NZ + t].astype(F32) + ya[t].astype(F32)
+        r = pl.ds(64 * j, 64)
+        if j == 0:
+            ya_put(t).wait_recv()
+        v = pa[y * NZ + t, r].astype(F32) + ya[t, r].astype(F32)
         if not (isinstance(k, int) and k == 0):
-            put(pa.at[0], ra.at[d, k - 1], ra_s.at[d, k - 1], ra_q.at[d, k - 1], ep=zr).wait_recv()
-            v = v + ra[d, k - 1].astype(F32)
-        pa[y * NZ + t] = v.astype(BF)
-        put(
-            pa.at[y * NZ + t], ra.at[d, k], ra_s.at[d, k], ra_q.at[d, k], ep=zr if d == 0 else zl
-        ).start()
-
-    def b_step(d, n, k):
+            a_put(d, k - 1, t, j).wait_recv()
+            v = v + ra[d, k - 1, r].astype(F32)
+        pa[y * NZ + t, r] = v.astype(BF)
+        a_put(d, k, t, j).start()
+
+    def b_step(d, n, k, j):
         t = target(d, n, k)
         if not (isinstance(k, int) and k == 0):
-            put(pb.at[0], rb.at[d, k - 1], rb_s.at[d, k - 1], rb_q.at[d, k - 1], ep=zr).wait_recv()
-            pb[t] = (pb[t].astype(F32) + rb[d, k - 1].astype(F32)).astype(BF)
-        put(pb.at[t], rb.at[d, k], rb_s.at[d, k], rb_q.at[d, k], ep=zr if d == 0 else zl).start()
+            b_put(d, k - 1, t, j).wait_recv()
+            pb[t, j] = (pb[t, j].astype(F32) + rb[d, k - 1, j].astype(F32)).astype(BF)
+        b_put(d, k, t, j).start()
 
     def all_steps(k):
-        b_step(0, 7, k)
-        b_step(1, 8, k)
-        a_step(0, 8, k)
-        a_step(1, 7, k)
+        for j in range(2):
+            b_step(0, 7, k, j)
+            b_step(1, 8, k, j)
+        for j in range(2):
+            a_step(0, 8, k, j)
+            a_step(1, 7, k, j)
 
     all_steps(0)
     loop(1, 7, all_steps)
-    b_step(1, 8, 7)
-    a_step(0, 8, 7)
-    put(pb.at[0], rb.at[0, 6], rb_s.at[0, 6], rb_q.at[0, 6], ep=zr).wait_recv()
-    put(pb.at[0], rb.at[1, 7], rb_s.at[1, 7], rb_q.at[1, 7], ep=zr).wait_recv()
+    for j in range(2):
+        b_step(1, 8, 7, j)
+    for j in range(2):
+        a_step(0, 8, 7, j)
+    for j in range(2):
+        b_put(0, 6, z, j).wait_recv()
+        b_put(1, 7, z, j).wait_recv()
     ag_own = (
         pb[z, y].astype(F32) + rb[0, 6, y].astype(F32) + rb[1, 7, y].astype(F32)
     )
@@ -258,9 +298,20 @@
     ).astype(BF)
     yb_put = put(pb.at[z, 1 - y], yb, yb_s, yb_q, ep=py)
     yb_put.start()
+
+    def ring_sends():
+        for d in range(2):
+            na, nb = (8, 7) if d == 0 else (7, 8)
+            for j in range(2):
+                loop(0, na, lambda k: a_put(d, k, z, j).wait_send())
+                loop(0, nb, lambda k: b_put(d, k, z, j).wait_send())
+        yb_put.wait_send()
+
+    tail.append(ring_sends)
     ya_put(z).wait_recv()
-    put(pa.at[0], ra.at[1, 6], ra_s.at[1, 6], ra_q.at[1, 6], ep=zr).wait_recv()
-    put(pa.at[0], ra.at[0, 7], ra_s.at[0, 7], ra_q.at[0, 7], ep=zr).wait_recv()
+    for j in range(2):
+        a_put(1, 6, z, j).wait_recv()
+        a_put(0, 7, z, j).wait_recv()
     pre = (
         pa[p].astype(F32) + ya[z].astype(F32) + ra[0, 7].astype(F32) + ra[1, 6].astype(F32)
     )
@@ -274,6 +325,7 @@
     ha[p, :, 0:128] = (ag * up * sg * (1.0 + gate * (1.0 - sg))).astype(BF)
     ha[p, :, 128:256] = (ag * gate * sg).astype(BF)
 
+    tail.append(hy_put.wait_send)
     def origin(d, k):
         return (z + NZ + (-k if d == 0 else k)) % NZ
 
@@ -321,6 +373,15 @@
     gb_step(1, 7)
     ga_step(0, 8, False)
     gb_step(1, 8, False)
+
+    def gather_sends():
+        for d in range(2):
+            na, nb = (8, 7) if d == 0 else (7, 8)
+            loop(0, na, lambda k: ga_put(d, k, z).wait_send())
+            loop(0, nb, lambda k: gb_put(d, k, z).wait_send())
+        loop(0, 16, lambda o: gy_put(y, o).wait_send())
+
+    tail.append(gather_sends)
 
     def spread_back(q):
         zp = q % 8
@@ -333,9 +394,9 @@
         )
         he[q] = mm(er[q], hq).astype(BF)
 
-    loop(0, 8, lambda i: spread_back(y * 8 + i))
+    dots(0, 8, lambda i: spread_back(y * 8 + i))
     loop(0, 16, lambda o: gy_put(1 - y, o).wait_recv())
-    loop(0, 8, lambda i: spread_back((1 - y) * 8 + i))
+    dots(0, 8, lambda i: spread_back((1 - y) * 8 + i))
 
     def back_dots(s):
         w = wall[host(s)]
@@ -344,7 +405,7 @@
         se[:, rows, 0:128] = mm(hs[:, 256:384], w[:, 256:384], LAST).astype(BF).reshape(16, 16, 128)
         se[:, rows, 128:256] = mm(hs[:, 0:256], w[:, 0:256], LAST).astype(BF).reshape(16, 16, 128)
 
-    loop(0, 32, back_dots)
+    dots(0, 32, back_dots, 1)
 
     def squeeze_out(q):
         cc = mm(et[q], se[q, :, 0:256]).astype(BF)
@@ -354,7 +415,7 @@
                     128 * i : 128 * (i + 1), 128 * kind : 128 * (kind + 1)
                 ].reshape(8, 16, 128)
 
-    loop(0, 16, squeeze_out)
+    dots(0, 16, squeeze_out)
 
     def c5(dx, h):
         i = 2 * dx + h
@@ -369,8 +430,16 @@
         rows = pl.ds(pl.multiple_of(s * 16, 16), 16)
         xd = xe[:, rows, :].reshape(256, 256)
         hs = he[:, rows, :].reshape(256, 384)
-        tot[s, :, 0:256] = mm(xd[:, 0:128], hs[:, 0:256], FIRST)[0:112].astype(BF).astype(F32)
-        tot[s, :, 256:384] = mm(xd[:, 128:256], hs[:, 256:384], FIRST)[0:112].astype(BF).astype(F32)
+        tot[s, :, 0:256] = mm(xd[:, 0:128], hs[:, 0:256], FIRST)[0:112].astype(BF)
+        tot[s, :, 256:384] = mm(xd[:, 128:256], hs[:, 256:384], FIRST)[0:112].astype(BF)
+
+    w_out = []
+
+    def weight_group(i):
+        dots(8 * i, 8 * i + 8, weight_dots, 1)
+        part = pl.ds(8 * i, 8)
+        w_out.append(pltpu.make_async_copy(tot.at[part], slots_ref.at[part], o_sem.at[i]))
+        w_out[-1].start()
 
     def addto(t, r):
         qq[t] = (qq[t].astype(F32) + r.astype(F32)).astype(BF)
@@ -388,7 +457,6 @@
             qq.at[gi(t, h, c)], rx.at[d, h], x5_s.at[d, h], x5_q.at[d, h], grp=gr if d == 0 else gl
         )
 
-    loop(0, 4, weight_dots)
     for h in range(2):
         with_core(2, h)
         f5(h).start()
@@ -404,7 +472,7 @@
     f5(1).wait_recv()
     addto(gi(xl, 1, c), rfar[1])
     x5(1, 1).start()
-    loop(4, 12, weight_dots)
+    weight_group(0)
     for h in range(2):
         c5(0, h).wait_recv()
         for d in range(2):
@@ -421,88 +489,94 @@
     qq[gy] = own_sum(1 - yh).astype(BF)
     y5 = put(qq.at[gy], ry, y5_s, y5_q, grp=gy)
     y5.start()
-    loop(12, 20, weight_dots)
+    weight_group(1)
     mine = own_sum(yh)
     y5.wait_recv()
     fin[...] = (mine + ry[...].astype(F32)).astype(BF)
 
-    b1 = lambda i, t: put(fin.at[t], b1r.at[p // 2, p % 2], b1_s.at[i], b1_q.at[i], ep=t)
-    b2 = lambda i, t: put(b1r.at[t], b2r.at[g], b2_s.at[i], b2_q.at[i], grp=t)
-    loop(1, NEP, lambda i: b1(i, (p + i) % NEP).start())
-    b1r[p // 2, p % 2] = fin[p]
-    loop(20, 32, weight_dots)
+    def grp_sends():
+        for h in range(2):
+            for dx in range(4):
+                c5(dx, h).wait_send()
+            f5(h).wait_send()
+            for d in range(2):
+                x5(d, h).wait_send()
+        y5.wait_send()
+
+    tail.append(grp_sends)
+    def b1(f):
+        return put(fin.at[f], b2r.at[g, p % 2], b1_s.at[f], b1_q.at[2 * g + p % 2], grp=p // 2, ep=f)
+
+    def b1_here(f):
+        return (p // 2 == g) & (f == p)
+
+    def b1_start(i):
+        f = (p + i) % NEP
+
+        @pl.when(jnp.logical_not(b1_here(f)))
+        def _():
+            b1(f).start()
+
+    loop(0, NEP, b1_start)
+
+    @pl.when(p // 2 == g)
+    def _():
+        b2r[g, p % 2] = fin[p]
+
+    weight_group(2)
+    weight_group(3)
 
     def b1_wait(i):
-        f = (p + NEP - i) % NEP
-        put(fin.at[0], b1r.at[f // 2, f % 2], b1_s.at[i], b1_q.at[i], ep=f).wait_recv()
-
-    loop(1, NEP, b1_wait)
-    loop(1, NGRP, lambda i: b2(i, (g + i) % NGRP).start())
-    b2r[g] = b1r[g]
-
-    def chain(j):
+        t, h = i // 2, i % 2
+
+        @pl.when(jnp.logical_not((t == g) & (2 * g + h == p)))
+        def _():
+            put(fin.at[0], b2r.at[t, h], b1_s.at[0], b1_q.at[i], grp=t, ep=2 * g + h).wait_recv()
+
+    def b1_left(f):
+        @pl.when(jnp.logical_not(b1_here(f)))
+        def _():
+            b1(f).wait_send()
+
+    tail.append(lambda: loop(0, NEP, b1_left))
+    loop(0, NEP, b1_wait)
+    rows_out = pltpu.make_async_copy(b2r, rows_ref, o_sem.at[4])
+    rows_out.start()
+    tail.append(rows_out.wait)
+    for grp4 in w_out:
+        tail.append(grp4.wait)
+
+    for wait in tail:
+        wait()
+
+
+def finish(rows_ref, slots_ref, rw_ref, hot_ref, out_ref, gtok_ref, gg_ref, gu_ref, gd_ref, acc):
+    def base(e, _):
+        acc[e] = slots_ref[e].astype(F32)
+        return 0
+
+    def more(j, _):
         e = hot_ref[j]
-
-        def look(i, prev):
-            return jnp.where((i < j) & (hot_ref[i] == e), 16 + i, prev)
-
-        prev = lax.fori_loop(0, 16, look, e)
-        tot[16 + j] = tot[16 + j] + tot[prev]
-
-    loop(0, 16, chain)
-
-    def close(e):
-        last = lax.fori_loop(0, 16, lambda i, v: jnp.where(hot_ref[i] == e, 16 + i, v), e)
-        v = tot[last].astype(BF)
-        for i in range(3):
-            go[i, e] = v[:, 128 * i : 128 * (i + 1)]
-
-    loop(0, 16, close)
-    w_out = [
-        pltpu.make_async_copy(go.at[i], r, o_sem.at[i]) for i, r in enumerate((gg_ref, gu_ref, gd_ref))
-    ]
-    for cp in w_out:
-        cp.start()
-
-    def b2_wait(i):
-        f = (g + NGRP - i) % NGRP
-        put(b1r.at[0], b2r.at[f], b2_s.at[i], b2_q.at[i], grp=f).wait_recv()
-
-    loop(1, NGRP, b2_wait)
+        acc[e] = acc[e] + slots_ref[16 + j].astype(F32)
+        return 0
+
+    def close(e, _):
+        v = acc[e].astype(BF)
+        gg_ref[e] = v[:, 0:128]
+        gu_ref[e] = v[:, 128:256]
+        gd_ref[e] = v[:, 256:384]
+        return 0
+
+    lax.fori_loop(0, 16, base, 0)
+    lax.fori_loop(0, 16, more, 0)
+    lax.fori_loop(0, 16, close, 0)
     for kind, ref in enumerate((out_ref, gtok_ref)):
         for h in range(2):
-            rows = b2r[kind * 8 : (kind + 1) * 8, h].reshape(128, 128).astype(F32)
-            v = jnp.transpose(rows)[0:112]
+            part = rows_ref[kind * 8 : (kind + 1) * 8, h].reshape(128, 128).astype(F32)
+            v = jnp.transpose(part)[0:112]
             if kind == 0:
-                v = v * rw_row
+                v = v * rw_ref[...]
             ref[h * 112 : (h + 1) * 112, :] = v.astype(BF)
-
-    loop(1, NGRP, lambda i: a1(i, (g + i) % NGRP).wait_send())
-    loop(1, NEP, lambda i: mt(i, (p + i) % NEP).wait_send())
-    loop(1, NEP, lambda i: a2(i, (p + i) % NEP).wait_send())
-    loop(0, 15, lambda i: g3(g, i, gy).wait_send())
-    loop(0, 16, lambda t: ya_put(t).wait_send())
-    for d in range(2):
-        na, nb = (8, 7) if d == 0 else (7, 8)
-        loop(0, na, lambda k: put(pa.at[0], ra.at[d, k], ra_s.at[d, k], ra_q.at[d, k], ep=zr).wait_send())
-        loop(0, nb, lambda k: put(pb.at[0], rb.at[d, k], rb_s.at[d, k], rb_q.at[d, k], ep=zr).wait_send())
-        loop(0, na, lambda k: ga_put(d, k, z).wait_send())
-        loop(0, nb, lambda k: gb_put(d, k, z).wait_send())
-    yb_put.wait_send()
-    hy_put.wait_send()
-    loop(0, 16, lambda o: gy_put(y, o).wait_send())
-    for dx in range(4):
-        for h in range(2):
-            c5(dx, h).wait_send()
-    for h in range(2):
-        f5(h).wait_send()
-        for d in range(2):
-            x5(d, h).wait_send()
-    y5.wait_send()
-    loop(1, NEP, lambda i: b1(i, (p + i) % NEP).wait_send())
-    loop(1, NGRP, lambda i: b2(i, (g + i) % NGRP).wait_send())
-    for cp in w_out:
-        cp.wait()
 
 
 def layer(tokens, routes, route_weights, hot_experts, w_gate, w_up, w_down, cotangent):
@@ -511,22 +585,20 @@
     vm = pl.BlockSpec(memory_space=pltpu.VMEM)
     anym = pl.BlockSpec(memory_space=pl.ANY)
     sems = [
-        (3,), (3,), (16,), (16,), (32,), (32,), (32,), (32,), (15,), (15,),
-        (16,), (16,), (2, 8), (2, 8), (2, 8), (2, 8), None, None,
+        (3,), (5,), (16,), (16,), (32,), (32,), (32,), (32,), (15,), (15,),
+        (16,), (16,), (2, 8, 2), (2, 8, 2), (2, 8, 2), (2, 8, 2), None, None,
         None, None, (2, 8), (2, 8), (2, 8), (2, 8), (16,), (16,),
-        (8,), (8,), (2,), (2,), (2, 2), (2, 2), None, None, (32,), (32,), (16,), (16,),
+        (8,), (8,), (2,), (2,), (2, 2), (2, 2), None, None, (32,), (32,),
     ]
-    out_t, gtok_t, gg, gu, gd = pl.pallas_call(
+    rw = route_weights.reshape(1, 128)
+    rows, slots = pl.pallas_call(
         body,
         out_shape=(
-            jax.ShapeDtypeStruct((224, 128), BF),
-            jax.ShapeDtypeStruct((224, 128), BF),
-            jax.ShapeDtypeStruct((16, 112, 128), BF),
-            jax.ShapeDtypeStruct((16, 112, 128), BF),
-            jax.ShapeDtypeStruct((16, 112, 128), BF),
+            jax.ShapeDtypeStruct((16, 2, 16, 128), BF),
+            jax.ShapeDtypeStruct((32, 112, 384), BF),
         ),
         in_specs=[vm, vm, vm, pl.BlockSpec(memory_space=pltpu.SMEM), anym, anym, anym, vm],
-        out_specs=(vm, vm, anym, anym, anym),
+        out_specs=(anym, anym),
         scratch_shapes=[
             v((16, 2, 16, 128), BF),
             v((32, 16, 128), BF),
@@ -553,9 +625,7 @@
             v((32, 16, 128), BF),
             v((32, 16, 128), BF),
             v((16, 2, 16, 128), BF),
-            v((16, 2, 16, 128), BF),
-            v((32, 112, 384), F32),
-            v((3, 16, 112, 128), BF),
+            v((32, 112, 384), BF),
         ]
         + [dma if s is None else dma(s) for s in sems],
         compiler_params=pltpu.CompilerParams(
@@ -565,13 +635,28 @@
     )(
         tokens.T,
         routes.reshape(1, 128),
-        route_weights.reshape(1, 128),
+        rw,
         hot_experts,
         w_gate,
         w_up,
         jnp.swapaxes(w_down, 1, 2),
         cotangent.T,
     )
+    grad = jax.ShapeDtypeStruct((16, 112, 128), BF)
+    out_t, gtok_t, gg, gu, gd = pl.pallas_call(
+        finish,
+        out_shape=(
+            jax.ShapeDtypeStruct((224, 128), BF),
+            jax.ShapeDtypeStruct((224, 128), BF),
+            grad,
+            grad,
+            grad,
+        ),
+        in_specs=[vm, vm, vm, pl.BlockSpec(memory_space=pltpu.SMEM)],
+        out_specs=(vm, vm, vm, vm, vm),
+        scratch_shapes=[v((16, 112, 384), F32)],
+        compiler_params=pltpu.CompilerParams(vmem_limit_bytes=32 * 1024 * 1024),
+    )(rows, slots, rw, hot_experts)
     return out_t.T, gtok_t.T, gg, gu, jnp.swapaxes(gd, 1, 2)
 
 

time: 194 us -> 188 us (0.969)
  the two profiles are of different devices: /device:TPU:1 before, /device:TPU:3 now
where the time goes in v2:
time: 188 us; the launch traced here: 187 us
  Pallas kernels  184 us (98%)
  local copies, waits for them, and re-layouts  2.68 us (1%)
    pallas_call x1, Pallas kernels, layer(): pl.pallas_call(body, out_shape=(jax.ShapeDtypeStruct((16, 2, 16, 128), BF...  182 us

profile of v2, /device:TPU:3, one launch (start us, length us, event | category | flops | bytes accessed | tf_op | source)
XLA Modules:
  0.0 187.5 jit_solution(13198537222585350175)
XLA Ops:
  0.6 0.0 copy-start.2
  0.6 0.0 copy-start.3
  0.7 181.7 %shard_map.119 = (bf16[16,2,16,128]{3,2,1,0:T(8,128)(2,1)}, bf16[32,112,384]{2,1,0:T(8,128)(2,1)}) custom-call(bf16[224,128]{1,0:T(8,128)(2,1)} %bitcast.12, s32[1,128]{1,0:T(1,128)} %bitcast.16, f32[1,128]{1,0:T(1,128)} %bitcast.8, s32[16]{0:T(128)} %hot_ref.3, bf16[16,112,128]{2,1,0:T(8,128)(2,1)} %wg_ref.1, bf16[16,112,128]{2,1,0:T(8,128)(2,1)} %wu_ref.1, ...), custom_call_target="tpu_custom_call" | custom-call | flops 8000000000 | bytes 3000000 | tf_op jit(solution)/shard_map/pallas_call | solution.py:594
  182.4 0.0 copy-done.2
  182.4 0.0 copy-done.3
  182.4 0.0 copy-start
  182.4 1.8 copy-done
  184.2 0.0 copy-start.1
  184.2 0.9 copy-done.1
  185.1 2.4 %shard_map.120 = (bf16[224,128]{1,0:T(8,128)(2,1)}, bf16[224,128]{1,0:T(8,128)(2,1)}, bf16[16,112,128]{2,1,0:T(8,128)(2,1)}, bf16[16,112,128]{2,1,0:T(8,128)(2,1)}, bf16[16,112,128]{2,1,0:T(8,128)(2,1)}) custom-call(bf16[16,2,16,128]{3,2,1,0:T(8,128)(2,1)S(1)} %copy-done.1, bf16[32,112,384]{2,1,0:T(8,128)(2,1)S(1)} %copy-done, f32[1,128]{1,0:T(1,128)S(1)} %bitcast.9, ...), custom_call_target="tpu_custom_call" | custom-call | tf_op jit(solution)/shard_map/pallas_call | solution.py:646
Async XLA Ops:
  0.6 181.8 %copy-start.2 = (f32[128,1]{0,1:T(1,128)S(1)}, f32[128,1]{0,1:T(1,128)}, u32[]{:S(2)}) copy-start(f32[128,1]{0,1:T(1,128)} %param.10) | copy-start | bytes 1540
  0.6 181.8 %copy-start.3 = (s32[16]{0:T(128)S(1)}, s32[16]{0:T(128)}, u32[]{:S(2)}) copy-start(s32[16]{0:T(128)} %hot_ref.3) | copy-start | bytes 196
  182.4 1.8 copy-start
  184.2 0.9 copy-start.1

commit v3 on v2

--- a/solution.py
+++ b/solution.py
@@ -197,31 +197,39 @@
     for cp in w_in:
         cp.wait()
 
-    def spread(q):
-        t0 = xb[:, 2 * q].reshape(256, 128)
-        t1 = xb[:, 2 * q + 1].reshape(256, 128)
-        xe[q] = mm(er[q], jnp.concatenate([t0, t1], axis=1), LAST).astype(BF)
-
-    dots(0, 16, spread)
+    def spread(i):
+        e = er[pl.ds(2 * i, 2)]
+        tb = xb[:, pl.ds(4 * i, 4)]
+        rows = []
+        for j in range(2):
+            t0, t1 = tb[:, 2 * j].reshape(256, 128), tb[:, 2 * j + 1].reshape(256, 128)
+            rows.append(mm(e[j], jnp.concatenate([t0, t1], axis=1), LAST).astype(BF))
+        xe[pl.ds(2 * i, 2)] = jnp.stack(rows)
+
+    dots(0, 8, spread)
 
     def host(s):
         return jnp.where(s < 16, s, hot_ref[jnp.maximum(s - 16, 0)])
 
-    def first_dots(s):
-        w = wall[host(s)]
-        rows = pl.ds(pl.multiple_of(s * 16, 16), 16)
-        xd = xe[:, rows, :].reshape(256, 256)
-        se[:, rows, 0:256] = mm(xd[:, 0:128], w[:, 0:256]).astype(BF).reshape(16, 16, 256)
-        se[:, rows, 256:384] = mm(xd[:, 128:256], w[:, 256:384]).astype(BF).reshape(16, 16, 128)
-
-    dots(0, 32, first_dots, 1)
-
-    def squeeze(q):
-        cc = mm(et[q], se[q]).astype(BF)
-        zp = q % 8
-        pa[pl.ds(2 * q, 2)] = cc[:, 0:256].reshape(2, 128, 256)
-        for i in range(2):
-            pb[2 * zp + i, q // 8] = cc[128 * i : 128 * (i + 1), 256:384]
+    def first_dots(i):
+        rows = pl.ds(pl.multiple_of(i * 64, 64), 64)
+        xd = xe[:, rows, :]
+        gu, dn = [], []
+        for j in range(4):
+            w = wall[host(4 * i + j)]
+            xj = xd[:, 16 * j : 16 * j + 16].reshape(256, 256)
+            gu.append(mm(xj[:, 0:128], w[:, 0:256]).astype(BF).reshape(16, 16, 256))
+            dn.append(mm(xj[:, 128:256], w[:, 256:384]).astype(BF).reshape(16, 16, 128))
+        se[:, rows, 0:256] = jnp.concatenate(gu, axis=1)
+        se[:, rows, 256:384] = jnp.concatenate(dn, axis=1)
+
+    dots(0, 8, first_dots, 1)
+
+    def squeeze(qs):
+        both = [mm(et[q], se[q]).astype(BF) for q in qs]
+        for q, cc in zip(qs, both):
+            pa[pl.ds(2 * q, 2)] = cc[:, 0:256].reshape(2, 128, 256)
+            pb[pl.ds(2 * (q % 8), 2), q // 8] = cc[:, 256:384].reshape(2, 128, 128)
 
     def ya_put(t):
         return put(pa.at[(1 - y) * NZ + t], ya.at[t], ya_s.at[t], ya_q.at[t], ep=py)
@@ -231,13 +239,14 @@
         return (z // 2 + off) % 8
 
     def squeeze_far(i):
-        zp = near(i)
-        squeeze((1 - y) * 8 + zp)
-        ya_put(2 * zp).start()
-        ya_put(2 * zp + 1).start()
-
-    dots(0, 8, squeeze_far)
-    dots(0, 8, lambda i: squeeze(y * 8 + near(i)))
+        zs = [near(2 * i + j) for j in range(2)]
+        squeeze([(1 - y) * 8 + zp for zp in zs])
+        for zp in zs:
+            ya_put(2 * zp).start()
+            ya_put(2 * zp + 1).start()
+
+    dots(0, 4, squeeze_far)
+    dots(0, 4, lambda i: squeeze([y * 8 + near(2 * i + j) for j in range(2)]))
     tail.append(lambda: loop(0, 16, lambda t: ya_put(t).wait_send()))
 
     def target(d, n, k):
@@ -383,39 +392,47 @@
 
     tail.append(gather_sends)
 
-    def spread_back(q):
-        zp = q % 8
-        hq = jnp.concatenate(
-            [
-                ha[pl.ds(2 * q, 2)].reshape(256, 256),
-                jnp.concatenate([hb[2 * zp, q // 8], hb[2 * zp + 1, q // 8]], axis=0),
-            ],
-            axis=1,
-        )
-        he[q] = mm(er[q], hq).astype(BF)
-
-    dots(0, 8, lambda i: spread_back(y * 8 + i))
+    def spread_back(i):
+        e = er[pl.ds(2 * i, 2)]
+        hs = ha[pl.ds(4 * i, 4)]
+        zp = (2 * i) % 8
+        hd = hb[pl.ds(2 * zp, 4), (2 * i) // 8]
+        rows = []
+        for j in range(2):
+            hq = jnp.concatenate(
+                [hs[2 * j : 2 * j + 2].reshape(256, 256), hd[2 * j : 2 * j + 2].reshape(256, 128)], axis=1
+            )
+            rows.append(mm(e[j], hq).astype(BF))
+        he[pl.ds(2 * i, 2)] = jnp.stack(rows)
+
+    dots(0, 4, lambda i: spread_back(y * 4 + i))
     loop(0, 16, lambda o: gy_put(1 - y, o).wait_recv())
-    dots(0, 8, lambda i: spread_back((1 - y) * 8 + i))
-
-    def back_dots(s):
-        w = wall[host(s)]
-        rows = pl.ds(pl.multiple_of(s * 16, 16), 16)
-        hs = he[:, rows, :].reshape(256, 384)
-        se[:, rows, 0:128] = mm(hs[:, 256:384], w[:, 256:384], LAST).astype(BF).reshape(16, 16, 128)
-        se[:, rows, 128:256] = mm(hs[:, 0:256], w[:, 0:256], LAST).astype(BF).reshape(16, 16, 128)
-
-    dots(0, 32, back_dots, 1)
-
-    def squeeze_out(q):
-        cc = mm(et[q], se[q, :, 0:256]).astype(BF)
-        for i in range(2):
-            for kind in range(2):
-                qq[kind * 8 : (kind + 1) * 8, 2 * q + i] = cc[
-                    128 * i : 128 * (i + 1), 128 * kind : 128 * (kind + 1)
-                ].reshape(8, 16, 128)
-
-    dots(0, 16, squeeze_out)
+    dots(0, 4, lambda i: spread_back((1 - y) * 4 + i))
+
+    def back_dots(i):
+        rows = pl.ds(pl.multiple_of(i * 64, 64), 64)
+        hs = he[:, rows, :]
+        dn, gu = [], []
+        for j in range(4):
+            w = wall[host(4 * i + j)]
+            hj = hs[:, 16 * j : 16 * j + 16].reshape(256, 384)
+            dn.append(mm(hj[:, 256:384], w[:, 256:384], LAST).astype(BF).reshape(16, 16, 128))
+            gu.append(mm(hj[:, 0:256], w[:, 0:256], LAST).astype(BF).reshape(16, 16, 128))
+        se[:, rows, 0:128] = jnp.concatenate(dn, axis=1)
+        se[:, rows, 128:256] = jnp.concatenate(gu, axis=1)
+
+    dots(0, 8, back_dots, 1)
+
+    def squeeze_out(i):
+        t = et[pl.ds(2 * i, 2)]
+        parts = se[pl.ds(2 * i, 2), :, 0:256]
+        sums = jnp.stack([mm(t[j], parts[j]).astype(BF) for j in range(2)])
+        sums = sums.reshape(4, 8, 16, 256)
+        for b in range(8):
+            qq[b, pl.ds(4 * i, 4)] = sums[:, b, :, 0:128]
+            qq[8 + b, pl.ds(4 * i, 4)] = sums[:, b, :, 128:256]
+
+    dots(0, 8, squeeze_out)
 
     def c5(dx, h):
         i = 2 * dx + h
@@ -426,17 +443,20 @@
         for h in range(2):
             c5(dx, h).start()
 
-    def weight_dots(s):
-        rows = pl.ds(pl.multiple_of(s * 16, 16), 16)
-        xd = xe[:, rows, :].reshape(256, 256)
-        hs = he[:, rows, :].reshape(256, 384)
-        tot[s, :, 0:256] = mm(xd[:, 0:128], hs[:, 0:256], FIRST)[0:112].astype(BF)
-        tot[s, :, 256:384] = mm(xd[:, 128:256], hs[:, 256:384], FIRST)[0:112].astype(BF)
+    def weight_dots(i):
+        rows = pl.ds(pl.multiple_of(i * 64, 64), 64)
+        xd = xe[:, rows, :]
+        hs = he[:, rows, :]
+        for j in range(4):
+            xj = xd[:, 16 * j : 16 * j + 16].reshape(256, 256)
+            hj = hs[:, 16 * j : 16 * j + 16].reshape(256, 384)
+            tot[4 * i + j, :, 0:256] = mm(xj[:, 0:128], hj[:, 0:256], FIRST)[0:112].astype(BF)
+            tot[4 * i + j, :, 256:384] = mm(xj[:, 128:256], hj[:, 256:384], FIRST)[0:112].astype(BF)
 
     w_out = []
 
     def weight_group(i):
-        dots(8 * i, 8 * i + 8, weight_dots, 1)
+        dots(2 * i, 2 * i + 2, weight_dots, 1)
         part = pl.ds(8 * i, 8)
         w_out.append(pltpu.make_async_copy(tot.at[part], slots_ref.at[part], o_sem.at[i]))
         w_out[-1].start()

time: 188 us -> 177 us (0.941)
  Pallas kernels: 184 us -> 173 us
    pallas_call x1, Pallas kernels: 182 us -> 171 us  [layer(): pl.pallas_call(body, out_shape=(jax.ShapeDtypeStruct((16, 2, 16, 128), BF...]
where the time goes in v3:
time: 177 us
  Pallas kernels  173 us (98%)
  local copies, waits for them, and re-layouts  2.68 us (2%)
    pallas_call x1, Pallas kernels, layer(): pl.pallas_call(body, out_shape=(jax.ShapeDtypeStruct((16, 2, 16, 128), BF...  171 us

profile of v3, /device:TPU:3, one launch (start us, length us, event | category | flops | bytes accessed | tf_op | source)
XLA Modules:
  0.0 176.5 jit_solution(16475394088580911110)
XLA Ops:
  0.6 0.0 copy-start.2
  0.6 0.0 copy-start.3
  0.7 170.8 %shard_map.119 = (bf16[16,2,16,128]{3,2,1,0:T(8,128)(2,1)}, bf16[32,112,384]{2,1,0:T(8,128)(2,1)}) custom-call(bf16[224,128]{1,0:T(8,128)(2,1)} %bitcast.12, s32[1,128]{1,0:T(1,128)} %bitcast.16, f32[1,128]{1,0:T(1,128)} %bitcast.8, s32[16]{0:T(128)} %hot_ref.3, bf16[16,112,128]{2,1,0:T(8,128)(2,1)} %wg_ref.1, bf16[16,112,128]{2,1,0:T(8,128)(2,1)} %wu_ref.1, ...), custom_call_target="tpu_custom_call" | custom-call | flops 8000000000 | bytes 3000000 | tf_op jit(solution)/shard_map/pallas_call | solution.py:614
  171.4 0.0 copy-done.2
  171.4 0.0 copy-done.3
  171.5 0.0 copy-start
  171.5 1.8 %copy-done = bf16[32,112,384]{2,1,0:T(8,128)(2,1)S(1)} copy-done((bf16[32,112,384]{2,1,0:T(8,128)(2,1)S(1)}, bf16[32,112,384]{2,1,0:T(8,128)(2,1)}, u32[]{:S(2)}) %copy-start) | copy-done | bytes 2752536
  173.2 0.0 copy-start.1
  173.2 0.9 copy-done.1
  174.1 2.4 %shard_map.120 = (bf16[224,128]{1,0:T(8,128)(2,1)}, bf16[224,128]{1,0:T(8,128)(2,1)}, bf16[16,112,128]{2,1,0:T(8,128)(2,1)}, bf16[16,112,128]{2,1,0:T(8,128)(2,1)}, bf16[16,112,128]{2,1,0:T(8,128)(2,1)}) custom-call(bf16[16,2,16,128]{3,2,1,0:T(8,128)(2,1)S(1)} %copy-done.1, bf16[32,112,384]{2,1,0:T(8,128)(2,1)S(1)} %copy-done, f32[1,128]{1,0:T(1,128)S(1)} %bitcast.9, ...), custom_call_target="tpu_custom_call" | custom-call | tf_op jit(solution)/shard_map/pallas_call | solution.py:666
Async XLA Ops:
  0.6 170.8 %copy-start.2 = (f32[128,1]{0,1:T(1,128)S(1)}, f32[128,1]{0,1:T(1,128)}, u32[]{:S(2)}) copy-start(f32[128,1]{0,1:T(1,128)} %param.10) | copy-start | bytes 1540
  0.6 170.8 %copy-start.3 = (s32[16]{0:T(128)S(1)}, s32[16]{0:T(128)}, u32[]{:S(2)}) copy-start(s32[16]{0:T(128)} %hot_ref.3) | copy-start | bytes 196
  171.5 1.8 %copy-start = (bf16[32,112,384]{2,1,0:T(8,128)(2,1)S(1)}, bf16[32,112,384]{2,1,0:T(8,128)(2,1)}, u32[]{:S(2)}) copy-start(bf16[32,112,384]{2,1,0:T(8,128)(2,1)} %get-tuple-element.13.slots_ref) | copy-start | bytes 8257540
  173.2 0.9 copy-start.1

commit v4 on v3

--- a/solution.py
+++ b/solution.py
@@ -101,7 +101,21 @@
 
     a1 = lambda i, t: put(src.at[t], a1r.at[g], a1_s.at[i], a1_q.at[i], grp=t)
     mt = lambda i, t: put(meta.at[p], meta.at[p], m_s.at[i], m_q.at[i], ep=t)
-    a2 = lambda i, t: put(a1r.at[t // 2, t % 2], xb.at[g, p], a2_s.at[i], a2_q.at[i], ep=t)
+
+    def place(at, yy, zz):
+        r = (zz + 2 * NZ - 2 * (at // 2 + 3)) % NZ
+        return r // 8, yy, r % 8
+
+    def a2(i, t):
+        return put(
+            a1r.at[t // 2, t % 2], xb.at[(g,) + place(t % NZ, y, z)], a2_s.at[i], a2_q.at[i], ep=t
+        )
+
+    def zpair(half, j):
+        return (z // 2 + 3 + 4 * half + j) % 8
+
+    def pair_block(q):
+        return ((q // 4) % 2) * NZ + 2 * zpair(q // 8, q % 4)
 
     def loop(lo, hi, f):
         def step(i, _):
@@ -130,7 +144,7 @@
     tail.append(lambda: loop(1, NGRP, lambda i: a1(i, (g + i) % NGRP).wait_send()))
     tail.append(lambda: loop(1, NEP, lambda i: mt(i, (p + i) % NEP).wait_send()))
     tail.append(lambda: loop(1, NEP, lambda i: a2(i, (p + i) % NEP).wait_send()))
-    xb[g, p] = a1r[p // 2, p % 2]
+    xb[(g,) + place(z, y, z)] = a1r[p // 2, p % 2]
 
     def m_wait(i):
         f = (p + NEP - i) % NEP
@@ -139,8 +153,8 @@
     loop(1, NEP, m_wait)
 
     def build(q):
-        m0 = meta[2 * q].astype(F32)
-        m1 = meta[2 * q + 1].astype(F32)
+        m0 = meta[pair_block(q)].astype(F32)
+        m1 = meta[pair_block(q) + 1].astype(F32)
         d0 = m0[0:1, :] * 16.0 + m0[1:2, :]
         d1 = m1[0:1, :] * 16.0 + m1[1:2, :] + 8.0
         row = jnp.concatenate([d0, d1], axis=1)
@@ -156,97 +170,100 @@
 
     def a2_wait(i):
         f = (p + NEP - i) % NEP
-        put(a1r.at[0, 0], xb.at[g, f], a2_s.at[i], a2_q.at[i], ep=f).wait_recv()
+        put(a1r.at[0, 0], xb.at[(g,) + place(z, f // NZ, f % NZ)], a2_s.at[i], a2_q.at[i], ep=f).wait_recv()
 
     dots(0, 4, build)
     loop(1, NEP, a2_wait)
 
-    def g3(chunk, i, t):
-        return put(xb.at[chunk], xb.at[chunk], g3_s.at[i], g3_q.at[i], grp=t)
-
-    g3(g, 0, gy).start()
-    g3(g, 1 + yh, gr).start()
-    g3(g, 3 + yh, gl).start()
-    g3(g, 7 + yh, gc).start()
-    dots(4, 8, build)
-    g3(gy, 0, gy).wait_recv()
-    g3(gy, 1 + (1 - yh), gr).start()
-    g3(gy, 3 + (1 - yh), gl).start()
-    g3(gy, 7 + (1 - yh), gc).start()
-    dots(8, 12, build)
+    def g3(chunk, i, t, k):
+        return put(xb.at[chunk, k], xb.at[chunk, k], g3_s.at[k, i], g3_q.at[k, i], grp=t)
+
     xf = (x + 2) % NX
-    g3(gi(xl, 0, c), 1, gr).wait_recv()
-    g3(gi(xl, 0, c), 5, gr).start()
-    g3(gi(xl, 0, c), 7 + 6, gc).start()
-    g3(gi(xr, 1, c), 4, gl).wait_recv()
-    g3(gi(xr, 1, c), 6, gl).start()
-    g3(gi(xr, 1, c), 7 + 3, gc).start()
-    g3(gi(xl, 1, c), 2, gr).wait_recv()
-    g3(gi(xl, 1, c), 7 + 7, gc).start()
-    g3(gi(xr, 0, c), 3, gl).wait_recv()
-    g3(gi(xr, 0, c), 7 + 2, gc).start()
-    dots(12, 16, build)
-    for h in range(2):
-        g3(gi(xf, h, c), 5 + h, gr).wait_recv()
-        g3(gi(xf, h, c), 7 + 4 + h, gc).start()
-    for dx in range(4):
+
+    def g_own(k):
+        g3(g, 1 + yh, gr, k).start()
+        g3(g, 3 + yh, gl, k).start()
+        g3(g, 7 + yh, gc, k).start()
+
+    def g_pair(k):
+        g3(gy, 0, gy, k).wait_recv()
+        g3(gy, 1 + (1 - yh), gr, k).start()
+        g3(gy, 3 + (1 - yh), gl, k).start()
+        g3(gy, 7 + (1 - yh), gc, k).start()
+
+    def g_relay(k):
+        g3(gi(xl, 0, c), 1, gr, k).wait_recv()
+        g3(gi(xl, 0, c), 5, gr, k).start()
+        g3(gi(xl, 0, c), 7 + 6, gc, k).start()
+        g3(gi(xr, 1, c), 4, gl, k).wait_recv()
+        g3(gi(xr, 1, c), 6, gl, k).start()
+        g3(gi(xr, 1, c), 7 + 3, gc, k).start()
+        g3(gi(xl, 1, c), 2, gr, k).wait_recv()
+        g3(gi(xl, 1, c), 7 + 7, gc, k).start()
+        g3(gi(xr, 0, c), 3, gl, k).wait_recv()
+        g3(gi(xr, 0, c), 7 + 2, gc, k).start()
+
+    def g_far(k):
         for h in range(2):
-            g3(gi((x + dx) % NX, h, 1 - c), 7 + 2 * dx + h, gc).wait_recv()
-
-    tail.append(lambda: loop(0, 15, lambda i: g3(g, i, gy).wait_send()))
-    for cp in w_in:
-        cp.wait()
+            g3(gi(xf, h, c), 5 + h, gr, k).wait_recv()
+            g3(gi(xf, h, c), 7 + 4 + h, gc, k).start()
+
+    def g_core(k):
+        for dx in range(4):
+            for h in range(2):
+                g3(gi((x + dx) % NX, h, 1 - c), 7 + 2 * dx + h, gc, k).wait_recv()
 
     def spread(i):
         e = er[pl.ds(2 * i, 2)]
-        tb = xb[:, pl.ds(4 * i, 4)]
+        k, yy, m = i // 4, (i // 2) % 2, i % 2
+        tb = xb[:, k, yy, pl.ds(4 * m, 4)]
         rows = []
         for j in range(2):
             t0, t1 = tb[:, 2 * j].reshape(256, 128), tb[:, 2 * j + 1].reshape(256, 128)
             rows.append(mm(e[j], jnp.concatenate([t0, t1], axis=1), LAST).astype(BF))
         xe[pl.ds(2 * i, 2)] = jnp.stack(rows)
 
-    dots(0, 8, spread)
-
     def host(s):
         return jnp.where(s < 16, s, hot_ref[jnp.maximum(s - 16, 0)])
 
-    def first_dots(i):
-        rows = pl.ds(pl.multiple_of(i * 64, 64), 64)
-        xd = xe[:, rows, :]
-        gu, dn = [], []
-        for j in range(4):
-            w = wall[host(4 * i + j)]
-            xj = xd[:, 16 * j : 16 * j + 16].reshape(256, 256)
-            gu.append(mm(xj[:, 0:128], w[:, 0:256]).astype(BF).reshape(16, 16, 256))
-            dn.append(mm(xj[:, 128:256], w[:, 256:384]).astype(BF).reshape(16, 16, 128))
-        se[:, rows, 0:256] = jnp.concatenate(gu, axis=1)
-        se[:, rows, 256:384] = jnp.concatenate(dn, axis=1)
-
-    dots(0, 8, first_dots, 1)
-
-    def squeeze(qs):
-        both = [mm(et[q], se[q]).astype(BF) for q in qs]
-        for q, cc in zip(qs, both):
-            pa[pl.ds(2 * q, 2)] = cc[:, 0:256].reshape(2, 128, 256)
-            pb[pl.ds(2 * (q % 8), 2), q // 8] = cc[:, 256:384].reshape(2, 128, 128)
+    def first_dots(k):
+        part = pl.ds(8 * k, 8)
+
+        def four(i):
+            rows = pl.ds(pl.multiple_of(i * 64, 64), 64)
+            xd = xe[part, rows, :]
+            gu, dn = [], []
+            for j in range(4):
+                w = wall[host(4 * i + j)]
+                xj = xd[:, 16 * j : 16 * j + 16].reshape(128, 256)
+                gu.append(mm(xj[:, 0:128], w[:, 0:256]).astype(BF).reshape(8, 16, 256))
+                dn.append(mm(xj[:, 128:256], w[:, 256:384]).astype(BF).reshape(8, 16, 128))
+            se[part, rows, 0:256] = jnp.concatenate(gu, axis=1)
+            se[part, rows, 256:384] = jnp.concatenate(dn, axis=1)
+
+        dots(0, 8, four, 1)
+
+    def squeeze(k, yy, i):
+        js = (1 - i, 2 + i) if k == 0 else (3 - i, i)
+        both = [mm(et[8 * k + 4 * yy + j], se[8 * k + 4 * yy + j]).astype(BF) for j in js]
+        for j, cc in zip(js, both):
+            zp = zpair(k, j)
+            pa[pl.ds(yy * NZ + 2 * zp, 2)] = cc[:, 0:256].reshape(2, 128, 256)
+            pb[pl.ds(2 * zp, 2), yy] = cc[:, 256:384].reshape(2, 128, 128)
+        return js
+
+    def squeezes(k):
+        def far(i):
+            for j in squeeze(k, 1 - y, i):
+                ya_put(2 * zpair(k, j)).start()
+                ya_put(2 * zpair(k, j) + 1).start()
+
+        loop(0, 2, far)
+        loop(0, 2, lambda i: squeeze(k, y, i))
 
     def ya_put(t):
         return put(pa.at[(1 - y) * NZ + t], ya.at[t], ya_s.at[t], ya_q.at[t], ep=py)
 
-    def near(i):
-        off = jnp.where(i % 2 == 1, 4 - (i + 1) // 2, 4 + i // 2)
-        return (z // 2 + off) % 8
-
-    def squeeze_far(i):
-        zs = [near(2 * i + j) for j in range(2)]
-        squeeze([(1 - y) * 8 + zp for zp in zs])
-        for zp in zs:
-            ya_put(2 * zp).start()
-            ya_put(2 * zp + 1).start()
-
-    dots(0, 4, squeeze_far)
-    dots(0, 4, lambda i: squeeze([y * 8 + near(2 * i + j) for j in range(2)]))
     tail.append(lambda: loop(0, 16, lambda t: ya_put(t).wait_send()))
 
     def target(d, n, k):
@@ -290,8 +307,39 @@
             a_step(0, 8, k, j)
             a_step(1, 7, k, j)
 
+    g3(g, 0, gy, 0).start()
+    g3(g, 0, gy, 1).start()
+    g_own(0)
+    dots(4, 10, build)
+    g_pair(0)
+    g_own(1)
+    dots(10, 16, build)
+    g_relay(0)
+    for cp in w_in:
+        cp.wait()
+    g_pair(1)
+    g_far(0)
+    for k in range(2):
+        tail.append(lambda k=k: loop(0, 15, lambda i: g3(g, i, gy, k).wait_send()))
+    g_core(0)
+    dots(0, 4, spread)
+    g_relay(1)
+    first_dots(0)
+    g_far(1)
+    squeezes(0)
     all_steps(0)
-    loop(1, 7, all_steps)
+    g_core(1)
+    dots(4, 8, spread)
+    first_dots(1)
+
+    def ring_and_rest(k):
+        all_steps(k)
+
+        @pl.when(k == 1)
+        def _():
+            squeezes(1)
+
+    loop(1, 7, ring_and_rest)
     for j in range(2):
         b_step(1, 8, 7, j)
     for j in range(2):
@@ -375,14 +423,6 @@
         gb_step(0, k)
         gb_step(1, k)
 
-    loop(1, 7, gather_steps)
-    ga_step(0, 7)
-    ga_step(1, 7, False)
-    gb_step(0, 7, False)
-    gb_step(1, 7)
-    ga_step(0, 8, False)
-    gb_step(1, 8, False)
-
     def gather_sends():
         for d in range(2):
             na, nb = (8, 7) if d == 0 else (7, 8)
@@ -392,56 +432,72 @@
 
     tail.append(gather_sends)
 
-    def spread_back(i):
-        e = er[pl.ds(2 * i, 2)]
-        hs = ha[pl.ds(4 * i, 4)]
-        zp = (2 * i) % 8
-        hd = hb[pl.ds(2 * zp, 4), (2 * i) // 8]
-        rows = []
-        for j in range(2):
-            hq = jnp.concatenate(
-                [hs[2 * j : 2 * j + 2].reshape(256, 256), hd[2 * j : 2 * j + 2].reshape(256, 128)], axis=1
-            )
-            rows.append(mm(e[j], hq).astype(BF))
-        he[pl.ds(2 * i, 2)] = jnp.stack(rows)
-
-    dots(0, 4, lambda i: spread_back(y * 4 + i))
-    loop(0, 16, lambda o: gy_put(1 - y, o).wait_recv())
-    dots(0, 4, lambda i: spread_back((1 - y) * 4 + i))
-
-    def back_dots(i):
-        rows = pl.ds(pl.multiple_of(i * 64, 64), 64)
-        hs = he[:, rows, :]
-        dn, gu = [], []
+    def spread_back(k):
+        def two(n):
+            yy, m = n // 2, n % 2
+            i = 8 * k + 2 * n
+            e = er[pl.ds(i, 2)]
+            rows = []
+            for j in range(2):
+                zp = zpair(k, 2 * m + j)
+                hq = jnp.concatenate(
+                    [
+                        ha[pl.ds(yy * NZ + 2 * zp, 2)].reshape(256, 256),
+                        hb[pl.ds(2 * zp, 2), yy].reshape(256, 128),
+                    ],
+                    axis=1,
+                )
+                rows.append(mm(e[j], hq).astype(BF))
+            he[pl.ds(i, 2)] = jnp.stack(rows)
+
+        loop(0, 4, two)
+
+    def gy_wait(k):
         for j in range(4):
-            w = wall[host(4 * i + j)]
-            hj = hs[:, 16 * j : 16 * j + 16].reshape(256, 384)
-            dn.append(mm(hj[:, 256:384], w[:, 256:384], LAST).astype(BF).reshape(16, 16, 128))
-            gu.append(mm(hj[:, 0:256], w[:, 0:256], LAST).astype(BF).reshape(16, 16, 128))
-        se[:, rows, 0:128] = jnp.concatenate(dn, axis=1)
-        se[:, rows, 128:256] = jnp.concatenate(gu, axis=1)
-
-    dots(0, 8, back_dots, 1)
-
-    def squeeze_out(i):
-        t = et[pl.ds(2 * i, 2)]
-        parts = se[pl.ds(2 * i, 2), :, 0:256]
-        sums = jnp.stack([mm(t[j], parts[j]).astype(BF) for j in range(2)])
-        sums = sums.reshape(4, 8, 16, 256)
-        for b in range(8):
-            qq[b, pl.ds(4 * i, 4)] = sums[:, b, :, 0:128]
-            qq[8 + b, pl.ds(4 * i, 4)] = sums[:, b, :, 128:256]
-
-    dots(0, 8, squeeze_out)
-
-    def c5(dx, h):
+            gy_put(1 - y, 2 * zpair(k, j)).wait_recv()
+            gy_put(1 - y, 2 * zpair(k, j) + 1).wait_recv()
+
+    def back_dots(k):
+        part = pl.ds(8 * k, 8)
+
+        def four(i):
+            rows = pl.ds(pl.multiple_of(i * 64, 64), 64)
+            hs = he[part, rows, :]
+            dn, gu = [], []
+            for j in range(4):
+                w = wall[host(4 * i + j)]
+                hj = hs[:, 16 * j : 16 * j + 16].reshape(128, 384)
+                dn.append(mm(hj[:, 256:384], w[:, 256:384], LAST).astype(BF).reshape(8, 16, 128))
+                gu.append(mm(hj[:, 0:256], w[:, 0:256], LAST).astype(BF).reshape(8, 16, 128))
+            se[part, rows, 0:128] = jnp.concatenate(dn, axis=1)
+            se[part, rows, 128:256] = jnp.concatenate(gu, axis=1)
+
+        dots(0, 8, four, 1)
+
+    def squeeze_out(k):
+        def two(i):
+            r = 8 * k + 2 * i
+            t = et[pl.ds(r, 2)]
+            parts = se[pl.ds(r, 2), :, 0:256]
+            sums = jnp.stack([mm(t[j], parts[j]).astype(BF) for j in range(2)])
+            sums = sums.reshape(4, 8, 16, 256)
+            m = pl.ds(4 * (i % 2), 4)
+            for b in range(8):
+                qq[b, k, i // 2, m] = sums[:, b, :, 0:128]
+                qq[8 + b, k, i // 2, m] = sums[:, b, :, 128:256]
+
+        dots(0, 4, two, 1)
+
+    def c5(dx, h, k):
         i = 2 * dx + h
-        return put(qq.at[gi((x + dx) % NX, h, 1 - c)], rc.at[i], c5_s.at[i], c5_q.at[i], grp=gc)
-
-    order = (2, 1, 3, 0)
-    for dx in order:
-        for h in range(2):
-            c5(dx, h).start()
+        return put(
+            qq.at[gi((x + dx) % NX, h, 1 - c), k], rc.at[k, i], c5_s.at[k, i], c5_q.at[k, i], grp=gc
+        )
+
+    def core_sends(k):
+        for dx in (2, 1, 3, 0):
+            for h in range(2):
+                c5(dx, h, k).start()
 
     def weight_dots(i):
         rows = pl.ds(pl.multiple_of(i * 64, 64), 64)
@@ -461,97 +517,146 @@
         w_out.append(pltpu.make_async_copy(tot.at[part], slots_ref.at[part], o_sem.at[i]))
         w_out[-1].start()
 
-    def addto(t, r):
-        qq[t] = (qq[t].astype(F32) + r.astype(F32)).astype(BF)
-
-    def with_core(dx, h):
-        c5(dx, h).wait_recv()
-        addto(gi((x + dx) % NX, h, c), rc[2 * dx + h])
-
-    def f5(h):
-        return put(qq.at[gi(xf, h, c)], rfar.at[h], f5_s.at[h], f5_q.at[h], grp=gr if h == 0 else gl)
-
-    def x5(d, h):
+    def addto(t, k, r):
+        qq[t, k] = (qq[t, k].astype(F32) + r.astype(F32)).astype(BF)
+
+    def with_core(dx, h, k):
+        c5(dx, h, k).wait_recv()
+        addto(gi((x + dx) % NX, h, c), k, rc[k, 2 * dx + h])
+
+    def f5(h, k):
+        return put(
+            qq.at[gi(xf, h, c), k], rfar.at[k, h], f5_s.at[k, h], f5_q.at[k, h], grp=gr if h == 0 else gl
+        )
+
+    def x5(d, h, k):
         t = xr if d == 0 else xl
         return put(
-            qq.at[gi(t, h, c)], rx.at[d, h], x5_s.at[d, h], x5_q.at[d, h], grp=gr if d == 0 else gl
-        )
-
-    for h in range(2):
-        with_core(2, h)
-        f5(h).start()
-    with_core(1, 1)
-    x5(0, 1).start()
-    with_core(3, 0)
-    x5(1, 0).start()
-    with_core(1, 0)
-    with_core(3, 1)
-    f5(0).wait_recv()
-    addto(gi(xr, 0, c), rfar[0])
-    x5(0, 0).start()
-    f5(1).wait_recv()
-    addto(gi(xl, 1, c), rfar[1])
-    x5(1, 1).start()
-    weight_group(0)
-    for h in range(2):
-        c5(0, h).wait_recv()
-        for d in range(2):
-            x5(d, h).wait_recv()
-
-    def own_sum(h):
+            qq.at[gi(t, h, c), k],
+            rx.at[k, d, h],
+            x5_s.at[k, d, h],
+            x5_q.at[k, d, h],
+            grp=gr if d == 0 else gl,
+        )
+
+    def x_first(k):
+        for h in range(2):
+            with_core(2, h, k)
+            f5(h, k).start()
+        with_core(1, 1, k)
+        x5(0, 1, k).start()
+        with_core(3, 0, k)
+        x5(1, 0, k).start()
+        with_core(1, 0, k)
+        with_core(3, 1, k)
+
+    def x_second(k):
+        f5(0, k).wait_recv()
+        addto(gi(xr, 0, c), k, rfar[k, 0])
+        x5(0, 0, k).start()
+        f5(1, k).wait_recv()
+        addto(gi(xl, 1, c), k, rfar[k, 1])
+        x5(1, 1, k).start()
+
+    def own_sum(h, k):
         return (
-            qq[gi(x, h, c)].astype(F32)
-            + rc[h].astype(F32)
-            + rx[0, h].astype(F32)
-            + rx[1, h].astype(F32)
-        )
-
-    qq[gy] = own_sum(1 - yh).astype(BF)
-    y5 = put(qq.at[gy], ry, y5_s, y5_q, grp=gy)
-    y5.start()
-    weight_group(1)
-    mine = own_sum(yh)
-    y5.wait_recv()
-    fin[...] = (mine + ry[...].astype(F32)).astype(BF)
+            qq[gi(x, h, c), k].astype(F32)
+            + rc[k, h].astype(F32)
+            + rx[k, 0, h].astype(F32)
+            + rx[k, 1, h].astype(F32)
+        )
+
+    def y5(k):
+        return put(qq.at[gy, k], ry.at[k], y5_s.at[k], y5_q.at[k], grp=gy)
+
+    def y_sends(k):
+        for h in range(2):
+            c5(0, h, k).wait_recv()
+            for d in range(2):
+                x5(d, h, k).wait_recv()
+        qq[gy, k] = own_sum(1 - yh, k).astype(BF)
+        y5(k).start()
+
+    def y_close(k):
+        y5(k).wait_recv()
+        fin[k] = (own_sum(yh, k) + ry[k].astype(F32)).astype(BF)
 
     def grp_sends():
-        for h in range(2):
-            for dx in range(4):
-                c5(dx, h).wait_send()
-            f5(h).wait_send()
-            for d in range(2):
-                x5(d, h).wait_send()
-        y5.wait_send()
+        for k in range(2):
+            for h in range(2):
+                for dx in range(4):
+                    c5(dx, h, k).wait_send()
+                f5(h, k).wait_send()
+                for d in range(2):
+                    x5(d, h, k).wait_send()
+            y5(k).wait_send()
 
     tail.append(grp_sends)
+
     def b1(f):
-        return put(fin.at[f], b2r.at[g, p % 2], b1_s.at[f], b1_q.at[2 * g + p % 2], grp=p // 2, ep=f)
+        return put(
+            fin.at[place(z, f // NZ, f % NZ)],
+            b2r.at[g, p % 2],
+            b1_s.at[f],
+            b1_q.at[2 * g + p % 2],
+            grp=p // 2,
+            ep=f,
+        )
 
     def b1_here(f):
         return (p // 2 == g) & (f == p)
 
     def b1_start(i):
-        f = (p + i) % NEP
+        f = ((i // 8) % 2) * NZ + (2 * zpair(i // 16, 0) + i % 8) % NZ
 
         @pl.when(jnp.logical_not(b1_here(f)))
         def _():
             b1(f).start()
 
-    loop(0, NEP, b1_start)
+    loop(1, 6, gather_steps)
+    gy_wait(1)
+    spread_back(1)
+    gather_steps(6)
+    back_dots(1)
+    ga_step(0, 7)
+    ga_step(1, 7, False)
+    gb_step(0, 7, False)
+    gb_step(1, 7)
+    squeeze_out(1)
+    core_sends(1)
+    ga_step(0, 8, False)
+    gb_step(1, 8, False)
+    x_first(1)
+    gy_wait(0)
+    spread_back(0)
+    x_second(1)
+    back_dots(0)
+    squeeze_out(0)
+    core_sends(0)
+    y_sends(1)
+    weight_group(0)
+    x_first(0)
+    y_close(1)
+    loop(16, 32, b1_start)
 
     @pl.when(p // 2 == g)
     def _():
-        b2r[g, p % 2] = fin[p]
-
+        b2r[g, p % 2] = fin[place(z, y, z)]
+
+    weight_group(1)
+    x_second(0)
     weight_group(2)
+    y_sends(0)
     weight_group(3)
+    y_close(0)
+    loop(0, 16, b1_start)
 
     def b1_wait(i):
         t, h = i // 2, i % 2
 
         @pl.when(jnp.logical_not((t == g) & (2 * g + h == p)))
         def _():
-            put(fin.at[0], b2r.at[t, h], b1_s.at[0], b1_q.at[i], grp=t, ep=2 * g + h).wait_recv()
+            put(fin.at[0, 0, 0], b2r.at[t, h], b1_s.at[0], b1_q.at[i], grp=t, ep=2 * g + h).wait_recv()
 
     def b1_left(f):
         @pl.when(jnp.logical_not(b1_here(f)))
@@ -605,10 +710,10 @@
     vm = pl.BlockSpec(memory_space=pltpu.VMEM)
     anym = pl.BlockSpec(memory_space=pl.ANY)
     sems = [
-        (3,), (5,), (16,), (16,), (32,), (32,), (32,), (32,), (15,), (15,),
+        (3,), (5,), (16,), (16,), (32,), (32,), (32,), (32,), (2, 15), (2, 15),
         (16,), (16,), (2, 8, 2), (2, 8, 2), (2, 8, 2), (2, 8, 2), None, None,
         None, None, (2, 8), (2, 8), (2, 8), (2, 8), (16,), (16,),
-        (8,), (8,), (2,), (2,), (2, 2), (2, 2), None, None, (32,), (32,),
+        (2, 8), (2, 8), (2, 2), (2, 2), (2, 2, 2), (2, 2, 2), (2,), (2,), (32,), (32,),
     ]
     rw = route_weights.reshape(1, 128)
     rows, slots = pl.pallas_call(
@@ -623,7 +728,7 @@
             v((16, 2, 16, 128), BF),
             v((32, 16, 128), BF),
             v((16, 2, 16, 128), BF),
-            v((16, 32, 16, 128), BF),
+            v((16, 2, 2, 8, 16, 128), BF),
             v((16, 512, 256), BF),
             v((16, 256, 512), BF),
             v((16, 128, 384), BF),
@@ -638,12 +743,12 @@
             v((32, 128, 256), BF),
             v((16, 2, 128, 128), BF),
             v((16, 512, 384), BF),
-            v((16, 32, 16, 128), BF),
-            v((8, 32, 16, 128), BF),
-            v((2, 32, 16, 128), BF),
-            v((2, 2, 32, 16, 128), BF),
-            v((32, 16, 128), BF),
-            v((32, 16, 128), BF),
+            v((16, 2, 2, 8, 16, 128), BF),
+            v((2, 8, 2, 8, 16, 128), BF),
+            v((2, 2, 2, 8, 16, 128), BF),
+            v((2, 2, 2, 2, 8, 16, 128), BF),
+            v((2, 2, 8, 16, 128), BF),
+            v((2, 2, 8, 16, 128), BF),
             v((16, 2, 16, 128), BF),
             v((32, 112, 384), BF),
         ]

time: 177 us -> 170 us (0.960)
  Pallas kernels: 173 us -> 165 us
    pallas_call x1, Pallas kernels: 171 us -> 162 us  [layer(): pl.pallas_call(body, out_shape=(jax.ShapeDtypeStruct((16, 2, 16, 128), BF...]
where the time goes in v4:
time: 170 us; the launch traced here: 168 us
  Pallas kernels  165 us (97%)
  local copies, waits for them, and re-layouts  2.68 us (2%)
    pallas_call x1, Pallas kernels, layer(): pl.pallas_call(body, out_shape=(jax.ShapeDtypeStruct((16, 2, 16, 128), BF...  162 us

profile of v4, /device:TPU:3, one launch (start us, length us, event | category | flops | bytes accessed | tf_op | source)
XLA Modules:
  0.0 168.0 jit_solution(14527155230994542059)
XLA Ops:
  0.6 0.0 copy-start.2
  0.6 0.0 copy-start.3
  0.7 162.2 %shard_map.119 = (bf16[16,2,16,128]{3,2,1,0:T(8,128)(2,1)}, bf16[32,112,384]{2,1,0:T(8,128)(2,1)}) custom-call(bf16[224,128]{1,0:T(8,128)(2,1)} %bitcast.12, s32[1,128]{1,0:T(1,128)} %bitcast.16, f32[1,128]{1,0:T(1,128)} %bitcast.8, s32[16]{0:T(128)} %hot_ref.3, bf16[16,112,128]{2,1,0:T(8,128)(2,1)} %wg_ref.1, bf16[16,112,128]{2,1,0:T(8,128)(2,1)} %wu_ref.1, ...), custom_call_target="tpu_custom_call" | custom-call | flops 8000000000 | bytes 3000000 | tf_op jit(solution)/shard_map/pallas_call | solution.py:719
  162.9 0.0 copy-done.2
  162.9 0.0 copy-done.3
  162.9 0.0 copy-start
  162.9 1.8 %copy-done = bf16[32,112,384]{2,1,0:T(8,128)(2,1)S(1)} copy-done((bf16[32,112,384]{2,1,0:T(8,128)(2,1)S(1)}, bf16[32,112,384]{2,1,0:T(8,128)(2,1)}, u32[]{:S(2)}) %copy-start) | copy-done | bytes 2752536
  164.7 0.0 copy-start.1
  164.7 0.9 copy-done.1
  165.6 2.4 %shard_map.120 = (bf16[224,128]{1,0:T(8,128)(2,1)}, bf16[224,128]{1,0:T(8,128)(2,1)}, bf16[16,112,128]{2,1,0:T(8,128)(2,1)}, bf16[16,112,128]{2,1,0:T(8,128)(2,1)}, bf16[16,112,128]{2,1,0:T(8,128)(2,1)}) custom-call(bf16[16,2,16,128]{3,2,1,0:T(8,128)(2,1)S(1)} %copy-done.1, bf16[32,112,384]{2,1,0:T(8,128)(2,1)S(1)} %copy-done, f32[1,128]{1,0:T(1,128)S(1)} %bitcast.9, ...), custom_call_target="tpu_custom_call" | custom-call | tf_op jit(solution)/shard_map/pallas_call | solution.py:771
Async XLA Ops:
  0.6 162.3 %copy-start.2 = (f32[128,1]{0,1:T(1,128)S(1)}, f32[128,1]{0,1:T(1,128)}, u32[]{:S(2)}) copy-start(f32[128,1]{0,1:T(1,128)} %param.10) | copy-start | bytes 1540
  0.6 162.3 %copy-start.3 = (s32[16]{0:T(128)S(1)}, s32[16]{0:T(128)}, u32[]{:S(2)}) copy-start(s32[16]{0:T(128)} %hot_ref.3) | copy-start | bytes 196
  162.9 1.8 %copy-start = (bf16[32,112,384]{2,1,0:T(8,128)(2,1)S(1)}, bf16[32,112,384]{2,1,0:T(8,128)(2,1)}, u32[]{:S(2)}) copy-start(bf16[32,112,384]{2,1,0:T(8,128)(2,1)} %get-tuple-element.13.slots_ref) | copy-start | bytes 8257540
  164.7 0.9 copy-start.1

commit v5 on v4

--- a/solution.py
+++ b/solution.py
@@ -325,9 +325,9 @@
     dots(0, 4, spread)
     g_relay(1)
     first_dots(0)
-    g_far(1)
     squeezes(0)
     all_steps(0)
+    g_far(1)
     g_core(1)
     dots(4, 8, spread)
     first_dots(1)
@@ -339,7 +339,15 @@
         def _():
             squeezes(1)
 
+        for at, waits in ((3, tail[0:3]), (4, tail[3:])):
+
+            @pl.when(k == at)
+            def _(waits=waits):
+                for wait in waits:
+                    wait()
+
     loop(1, 7, ring_and_rest)
+    tail.clear()
     for j in range(2):
         b_step(1, 8, 7, j)
     for j in range(2):
@@ -430,8 +438,6 @@
             loop(0, nb, lambda k: gb_put(d, k, z).wait_send())
         loop(0, 16, lambda o: gy_put(y, o).wait_send())
 
-    tail.append(gather_sends)
-
     def spread_back(k):
         def two(n):
             yy, m = n // 2, n % 2
@@ -591,8 +597,6 @@
                     x5(d, h, k).wait_send()
             y5(k).wait_send()
 
-    tail.append(grp_sends)
-
     def b1(f):
         return put(
             fin.at[place(z, f // NZ, f % NZ)],
@@ -613,7 +617,17 @@
         def _():
             b1(f).start()
 
-    loop(1, 6, gather_steps)
+    early, tail[:] = tail[:], []
+
+    def gather_and_rest(k):
+        gather_steps(k)
+
+        @pl.when(k == 2)
+        def _():
+            for wait in early:
+                wait()
+
+    loop(1, 6, gather_and_rest)
     gy_wait(1)
     spread_back(1)
     gather_steps(6)
@@ -633,6 +647,7 @@
     back_dots(0)
     squeeze_out(0)
     core_sends(0)
+    gather_sends()
     y_sends(1)
     weight_group(0)
     x_first(0)
@@ -663,7 +678,8 @@
         def _():
             b1(f).wait_send()
 
-    tail.append(lambda: loop(0, NEP, b1_left))
+    grp_sends()
+    loop(0, NEP, b1_left)
     loop(0, NEP, b1_wait)
     rows_out = pltpu.make_async_copy(b2r, rows_ref, o_sem.at[4])
     rows_out.start()
@@ -675,14 +691,23 @@
         wait()
 
 
-def finish(rows_ref, slots_ref, rw_ref, hot_ref, out_ref, gtok_ref, gg_ref, gu_ref, gd_ref, acc):
+def finish(
+    rows_ref, slots_ref, rw_ref, hot_ref, out_ref, gtok_ref, gg_ref, gu_ref, gd_ref, rows_v, slots_v, acc, sem
+):
+    rows_in = pltpu.make_async_copy(rows_ref, rows_v, sem.at[0])
+    low = pltpu.make_async_copy(slots_ref.at[pl.ds(0, 16)], slots_v.at[pl.ds(0, 16)], sem.at[1])
+    high = pltpu.make_async_copy(slots_ref.at[pl.ds(16, 16)], slots_v.at[pl.ds(16, 16)], sem.at[2])
+    rows_in.start()
+    low.start()
+    high.start()
+
     def base(e, _):
-        acc[e] = slots_ref[e].astype(F32)
+        acc[e] = slots_v[e].astype(F32)
         return 0
 
     def more(j, _):
         e = hot_ref[j]
-        acc[e] = acc[e] + slots_ref[16 + j].astype(F32)
+        acc[e] = acc[e] + slots_v[16 + j].astype(F32)
         return 0
 
     def close(e, _):
@@ -692,16 +717,19 @@
         gd_ref[e] = v[:, 256:384]
         return 0
 
-    lax.fori_loop(0, 16, base, 0)
-    lax.fori_loop(0, 16, more, 0)
-    lax.fori_loop(0, 16, close, 0)
+    rows_in.wait()
     for kind, ref in enumerate((out_ref, gtok_ref)):
         for h in range(2):
-            part = rows_ref[kind * 8 : (kind + 1) * 8, h].reshape(128, 128).astype(F32)
+            part = rows_v[kind * 8 : (kind + 1) * 8, h].reshape(128, 128).astype(F32)
             v = jnp.transpose(part)[0:112]
             if kind == 0:
                 v = v * rw_ref[...]
             ref[h * 112 : (h + 1) * 112, :] = v.astype(BF)
+    low.wait()
+    lax.fori_loop(0, 16, base, 0)
+    high.wait()
+    lax.fori_loop(0, 16, more, 0)
+    lax.fori_loop(0, 16, close, 0)
 
 
 def layer(tokens, routes, route_weights, hot_experts, w_gate, w_up, w_down, cotangent):
@@ -777,10 +805,15 @@
             grad,
             grad,
         ),
-        in_specs=[vm, vm, vm, pl.BlockSpec(memory_space=pltpu.SMEM)],
+        in_specs=[anym, anym, vm, pl.BlockSpec(memory_space=pltpu.SMEM)],
         out_specs=(vm, vm, vm, vm, vm),
-        scratch_shapes=[v((16, 112, 384), F32)],
-        compiler_params=pltpu.CompilerParams(vmem_limit_bytes=32 * 1024 * 1024),
+        scratch_shapes=[
+            v((16, 2, 16, 128), BF),
+            v((32, 112, 384), BF),
+            v((16, 112, 384), F32),
+            dma((3,)),
+        ],
+        compiler_params=pltpu.CompilerParams(vmem_limit_bytes=60 * 1024 * 1024),
     )(rows, slots, rw, hot_experts)
     return out_t.T, gtok_t.T, gg, gu, jnp.swapaxes(gd, 1, 2)
 

time: 170 us -> 168 us (0.988)
  local copies, waits for them, and re-layouts: 2.68 us -> 0 us
    unnamed x8 -> x0, local copies, waits for them, and re-layouts: 2.68 us -> none
    pallas_call x1, Pallas kernels: 2.39 us -> 4.27 us  [layer(): pl.pallas_call(finish, out_shape=(jax.ShapeDtypeStruct((224, 128), BF), j...]
where the time goes in v5:
time: 168 us; the launch traced here: 167 us
  Pallas kernels  166 us (99%)
    pallas_call x1, Pallas kernels, layer(): pl.pallas_call(body, out_shape=(jax.ShapeDtypeStruct((16, 2, 16, 128), BF...  162 us
    pallas_call x1, Pallas kernels, layer(): pl.pallas_call(finish, out_shape=(jax.ShapeDtypeStruct((224, 128), BF), j...  4.27 us

profile of v5, /device:TPU:3, one launch (start us, length us, event | category | flops | bytes accessed | tf_op | source)
XLA Modules:
  0.0 166.8 jit_solution(14516282389024804116)
XLA Ops:
  0.6 161.9 %shard_map.119 = (bf16[16,2,16,128]{3,2,1,0:T(8,128)(2,1)}, bf16[32,112,384]{2,1,0:T(8,128)(2,1)}) custom-call(bf16[224,128]{1,0:T(8,128)(2,1)} %bitcast.12, s32[1,128]{1,0:T(1,128)} %bitcast.16, f32[1,128]{1,0:T(1,128)} %bitcast.8, s32[16]{0:T(128)} %hot_ref.3, bf16[16,112,128]{2,1,0:T(8,128)(2,1)} %wg_ref.1, bf16[16,112,128]{2,1,0:T(8,128)(2,1)} %wu_ref.1, ...), custom_call_target="tpu_custom_call" | custom-call | flops 8000000000 | bytes 3000000 | tf_op jit(solution)/shard_map/pallas_call | solution.py:747
  162.5 4.3 %shard_map.120 = (bf16[224,128]{1,0:T(8,128)(2,1)}, bf16[224,128]{1,0:T(8,128)(2,1)}, bf16[16,112,128]{2,1,0:T(8,128)(2,1)}, bf16[16,112,128]{2,1,0:T(8,128)(2,1)}, bf16[16,112,128]{2,1,0:T(8,128)(2,1)}) custom-call(bf16[16,2,16,128]{3,2,1,0:T(8,128)(2,1)} %get-tuple-element.12.rows_ref, bf16[32,112,384]{2,1,0:T(8,128)(2,1)} %get-tuple-element.13.slots_ref, ...), custom_call_target="tpu_custom_call" | custom-call | tf_op jit(solution)/shard_map/pallas_call | solution.py:799

commit v6 on v5

--- a/solution.py
+++ b/solution.py
@@ -106,10 +106,15 @@
         r = (zz + 2 * NZ - 2 * (at // 2 + 3)) % NZ
         return r // 8, yy, r % 8
 
-    def a2(i, t):
+    def a2(t):
         return put(
-            a1r.at[t // 2, t % 2], xb.at[(g,) + place(t % NZ, y, z)], a2_s.at[i], a2_q.at[i], ep=t
-        )
+            a1r.at[t // 2, t % 2], xb.at[(g,) + place(t % NZ, y, z)], a2_s.at[t], a2_q.at[p], ep=t
+        )
+
+    def a2_start(n):
+        m = n // 2
+        off = jnp.where(m % 2 == 0, 8 - m // 2, 8 + (m + 1) // 2)
+        a2(((y + n) % 2) * NZ + (z + off) % NZ).start()
 
     def zpair(half, j):
         return (z // 2 + 3 + 4 * half + j) % 8
@@ -140,10 +145,11 @@
         put(src.at[f], a1r.at[f], a1_s.at[i], a1_q.at[i], grp=f).wait_recv()
 
     loop(1, NGRP, a1_wait)
-    loop(1, NEP, lambda i: a2(i, (p + i) % NEP).start())
+    loop(0, 30, a2_start)
+    a2(py).start()
     tail.append(lambda: loop(1, NGRP, lambda i: a1(i, (g + i) % NGRP).wait_send()))
     tail.append(lambda: loop(1, NEP, lambda i: mt(i, (p + i) % NEP).wait_send()))
-    tail.append(lambda: loop(1, NEP, lambda i: a2(i, (p + i) % NEP).wait_send()))
+    tail.append(lambda: loop(1, NEP, lambda i: a2((p + i) % NEP).wait_send()))
     xb[(g,) + place(z, y, z)] = a1r[p // 2, p % 2]
 
     def m_wait(i):
@@ -170,7 +176,7 @@
 
     def a2_wait(i):
         f = (p + NEP - i) % NEP
-        put(a1r.at[0, 0], xb.at[(g,) + place(z, f // NZ, f % NZ)], a2_s.at[i], a2_q.at[i], ep=f).wait_recv()
+        put(a1r.at[0, 0], xb.at[(g,) + place(z, f // NZ, f % NZ)], a2_s.at[f], a2_q.at[f], ep=f).wait_recv()
 
     dots(0, 4, build)
     loop(1, NEP, a2_wait)
@@ -330,13 +336,13 @@
     g_far(1)
     g_core(1)
     dots(4, 8, spread)
-    first_dots(1)
 
     def ring_and_rest(k):
         all_steps(k)
 
         @pl.when(k == 1)
         def _():
+            first_dots(1)
             squeezes(1)
 
         for at, waits in ((3, tail[0:3]), (4, tail[3:])):

time: 168 us -> 167 us (level)
  no operation moved by 1% of the time
where the time goes in v6:
time: 167 us; the launch traced here: 166 us
  Pallas kernels  166 us (99%)
    pallas_call x1, Pallas kernels, layer(): pl.pallas_call(body, out_shape=(jax.ShapeDtypeStruct((16, 2, 16, 128), BF...  161 us
    pallas_call x1, Pallas kernels, layer(): pl.pallas_call(finish, out_shape=(jax.ShapeDtypeStruct((224, 128), BF), j...  4.27 us

profile of v6, /device:TPU:3, one launch (start us, length us, event | category | flops | bytes accessed | tf_op | source)
XLA Modules:
  0.0 166.1 jit_solution(12898161056735596143)
XLA Ops:
  0.6 161.2 %shard_map.119 = (bf16[16,2,16,128]{3,2,1,0:T(8,128)(2,1)}, bf16[32,112,384]{2,1,0:T(8,128)(2,1)}) custom-call(bf16[224,128]{1,0:T(8,128)(2,1)} %bitcast.12, s32[1,128]{1,0:T(1,128)} %bitcast.16, f32[1,128]{1,0:T(1,128)} %bitcast.8, s32[16]{0:T(128)} %hot_ref.3, bf16[16,112,128]{2,1,0:T(8,128)(2,1)} %wg_ref.1, bf16[16,112,128]{2,1,0:T(8,128)(2,1)} %wu_ref.1, ...), custom_call_target="tpu_custom_call" | custom-call | flops 8000000000 | bytes 3000000 | tf_op jit(solution)/shard_map/pallas_call | solution.py:753
  161.9 4.3 %shard_map.120 = (bf16[224,128]{1,0:T(8,128)(2,1)}, bf16[224,128]{1,0:T(8,128)(2,1)}, bf16[16,112,128]{2,1,0:T(8,128)(2,1)}, bf16[16,112,128]{2,1,0:T(8,128)(2,1)}, bf16[16,112,128]{2,1,0:T(8,128)(2,1)}) custom-call(bf16[16,2,16,128]{3,2,1,0:T(8,128)(2,1)} %get-tuple-element.12.rows_ref, bf16[32,112,384]{2,1,0:T(8,128)(2,1)} %get-tuple-element.13.slots_ref, ...), custom_call_target="tpu_custom_call" | custom-call | tf_op jit(solution)/shard_map/pallas_call | solution.py:805

commit v7 on v6

--- a/solution.py
+++ b/solution.py
@@ -732,10 +732,10 @@
                 v = v * rw_ref[...]
             ref[h * 112 : (h + 1) * 112, :] = v.astype(BF)
     low.wait()
-    lax.fori_loop(0, 16, base, 0)
+    lax.fori_loop(0, 16, base, 0, unroll=4)
     high.wait()
-    lax.fori_loop(0, 16, more, 0)
-    lax.fori_loop(0, 16, close, 0)
+    lax.fori_loop(0, 16, more, 0, unroll=2)
+    lax.fori_loop(0, 16, close, 0, unroll=4)
 
 
 def layer(tokens, routes, route_weights, hot_experts, w_gate, w_up, w_down, cotangent):

time: 167 us -> 166 us (level)
  no operation moved by 1% of the time
where the time goes in v7:
time: 166 us
  Pallas kernels  165 us (99%)
    pallas_call x1, Pallas kernels, layer(): pl.pallas_call(body, out_shape=(jax.ShapeDtypeStruct((16, 2, 16, 128), BF...  161 us
    pallas_call x1, Pallas kernels, layer(): pl.pallas_call(finish, out_shape=(jax.ShapeDtypeStruct((224, 128), BF), j...  4.18 us

profile of v7, /device:TPU:3, one launch (start us, length us, event | category | flops | bytes accessed | tf_op | source)
XLA Modules:
  0.0 166.1 jit_solution(5311252319756556401)
XLA Ops:
  0.6 161.2 %shard_map.119 = (bf16[16,2,16,128]{3,2,1,0:T(8,128)(2,1)}, bf16[32,112,384]{2,1,0:T(8,128)(2,1)}) custom-call(bf16[224,128]{1,0:T(8,128)(2,1)} %bitcast.12, s32[1,128]{1,0:T(1,128)} %bitcast.16, f32[1,128]{1,0:T(1,128)} %bitcast.8, s32[16]{0:T(128)} %hot_ref.3, bf16[16,112,128]{2,1,0:T(8,128)(2,1)} %wg_ref.1, bf16[16,112,128]{2,1,0:T(8,128)(2,1)} %wu_ref.1, ...), custom_call_target="tpu_custom_call" | custom-call | flops 8000000000 | bytes 3000000 | tf_op jit(solution)/shard_map/pallas_call | solution.py:753
  161.9 4.2 %shard_map.120 = (bf16[224,128]{1,0:T(8,128)(2,1)}, bf16[224,128]{1,0:T(8,128)(2,1)}, bf16[16,112,128]{2,1,0:T(8,128)(2,1)}, bf16[16,112,128]{2,1,0:T(8,128)(2,1)}, bf16[16,112,128]{2,1,0:T(8,128)(2,1)}) custom-call(bf16[16,2,16,128]{3,2,1,0:T(8,128)(2,1)} %get-tuple-element.12.rows_ref, bf16[32,112,384]{2,1,0:T(8,128)(2,1)} %get-tuple-element.13.slots_ref, ...), custom_call_target="tpu_custom_call" | custom-call | tf_op jit(solution)/shard_map/pallas_call | solution.py:805
